TPU v7x, 32 devices: a whole 2x2x4 slice. The times are simulated.
32 devices in a mesh: tm: 4 (over y, core), space: 4 (over z), dp: 2 (over x).
Axes of the slice: x: 2, y: 2, z: 4, core: 2. Of those that a mesh axis runs over, the one named last changes fastest.
Arguments:
- latents: bfloat16 [2, 1024, 2048], P('dp', 'tm'), may hold values from -6 to 6
- proj_input: bfloat16 [2048, 128], replicated, may hold values from -0.125 to 0.125
- proj_output: bfloat16 [2048, 128], replicated, may hold values from -0.125 to 0.125
- scan_input: bfloat16 [2, 1024, 4096], P('dp', 'tm', 'space'), may hold values from -6 to 6
- log_decay: float32 [2, 1024, 32], P('dp', 'tm', 'space'), may hold values from -2 to 0
- att_queries: bfloat16 [2, 1024, 4096], P('dp', 'tm', 'space'), may hold values from -67.88225 to 67.88225
- att_keys: bfloat16 [2, 1024, 4096], P('dp', 'tm', 'space'), may hold values from -3 to 3
- att_values: bfloat16 [2, 1024, 4096], P('dp', 'tm', 'space'), may hold values from -6 to 6
- scan_cotangent: bfloat16 [2, 1024, 4096], P('dp', 'tm', 'space'), may hold values from -0.59765625 to 0.59765625
- window_offsets: int32 [2, 8], P('dp', 'tm'), may hold values from 0 to 63
Outputs:
- layer_out: bfloat16 [2, 1024, 4096], P('dp', 'tm', 'space')
- input_grad: bfloat16 [2, 1024, 4096], P('dp', 'tm', 'space')
- proj_grad: float32 [2048, 256], P('space')
All inputs are finite; a program needn't handle non-finite values.
Results may differ from a plain program's by a relative error of at most 0.027.
Values may be sent and summed in bfloat16 or wider, within the bound.
A program may use at most 64 MiB of HBM per device.

v0:
```python
import math

import jax
import jax.numpy as jnp
from jax import lax
from jax.sharding import PartitionSpec as P

W = 128
QB = 128


precise = lax.Precision.HIGHEST


def shifted(block, axis, distance):
    devices = range(lax.axis_size(axis))
    route = [(i - distance, i) for i in devices if i - distance in devices]
    return lax.ppermute(block, axis, route)


def block_decay(cum_decay):
    row_count = cum_decay.shape[1]
    position = jnp.arange(row_count)
    lower_mask = position[:, None] >= position[None, :]
    per_head_split = jnp.swapaxes(cum_decay, 1, 2)
    log_gap = per_head_split[:, :, :, None] - per_head_split[:, :, None, :]
    return jnp.exp(jnp.where(lower_mask, log_gap, -jnp.inf))


def on_device(
    latents,
    proj_input,
    proj_output,
    scan_input,
    log_decay,
    att_queries,
    att_keys,
    att_values,
    scan_cotangent,
    window_offsets,
):
    clip_count, row_count, model_width = latents.shape
    head_count = log_decay.shape[2]
    head_dim = scan_input.shape[2] // head_count
    state_count = proj_input.shape[1]
    state_scale = 1.0 / math.sqrt(state_count)
    b_rows = jnp.einsum(
        "crd,dn->crn", latents, proj_input, preferred_element_type=jnp.float32
    ).astype(jnp.bfloat16)
    c_rows = jnp.einsum(
        "crd,dn->crn", latents, proj_output, preferred_element_type=jnp.float32
    ).astype(jnp.bfloat16)
    cum_decay = jnp.cumsum(log_decay, axis=1)
    block_total = cum_decay[:, -1]
    head_rise = jnp.exp(cum_decay)
    tail_fall = jnp.exp(block_total[:, None] - cum_decay)
    decay_mat = block_decay(cum_decay)
    kernel = (
        jnp.einsum("ctn,csn->cts", c_rows, b_rows, preferred_element_type=jnp.float32) * state_scale
    )
    mixing = (kernel[:, None] * decay_mat).astype(jnp.bfloat16)
    scan_heads = scan_input.reshape(clip_count, row_count, head_count, head_dim)
    cotan_heads = scan_cotangent.reshape(clip_count, row_count, head_count, head_dim)
    scan_wide = scan_heads.astype(jnp.float32)
    cotan_wide = cotan_heads.astype(jnp.float32)
    b_wide = b_rows.astype(jnp.float32)
    c_wide = c_rows.astype(jnp.float32) * state_scale
    fresh = jnp.einsum(
        "cshp,csn->chpn", scan_wide * tail_fall[..., None], b_wide, precision=precise
    )
    back_fresh = jnp.einsum(
        "cthp,ctn->chpn", cotan_wide * head_rise[..., None], c_wide, precision=precise
    )
    carried = jnp.exp(block_total)

    def forward_step(counter, state):
        return shifted(
            (carried[..., None, None] * state + fresh).astype(jnp.bfloat16), "tm", 1
        ).astype(jnp.float32)

    def reverse_pass_step(counter, state):
        return shifted(
            (carried[..., None, None] * state + back_fresh).astype(jnp.bfloat16), "tm", -1
        ).astype(jnp.float32)

    state_in = lax.fori_loop(0, lax.axis_size("tm") - 1, forward_step, jnp.zeros_like(fresh))
    grad_in = lax.fori_loop(
        0, lax.axis_size("tm") - 1, reverse_pass_step, jnp.zeros_like(back_fresh)
    )
    tails = shifted((att_keys[:, row_count - W :], att_values[:, row_count - W :]), "tm", 1)
    inner = jnp.einsum("chts,cshp->cthp", mixing, scan_heads, preferred_element_type=jnp.float32)
    scan_out = inner + head_rise[..., None] * jnp.einsum(
        "ctn,chpn->cthp", c_wide, state_in, precision=precise
    )
    normed = scan_out * lax.rsqrt(jnp.mean(scan_out * scan_out, axis=-1, keepdims=True) + 1e-05)
    key_ext = jnp.concatenate([tails[0], att_keys], axis=1).reshape(
        clip_count, W + row_count, head_count, head_dim
    )
    value_ext = jnp.concatenate([tails[1], att_values], axis=1).reshape(
        clip_count, W + row_count, head_count, head_dim
    )
    query_heads = att_queries.reshape(clip_count, row_count, head_count, head_dim)
    start = lax.axis_index("tm") * row_count
    t_pos = start + jnp.arange(row_count)
    s_pos = start - W + jnp.arange(W + row_count)
    offset_each = jnp.repeat(window_offsets, QB, axis=1)
    seen = (
        (s_pos[None, None, :] <= t_pos[None, :, None])
        & (s_pos[None, None, :] >= t_pos[None, :, None] - W + 1 + offset_each[:, :, None])
        & (s_pos[None, None, :] >= 0)
    )
    scores = jnp.einsum(
        "cthp,cshp->chts", query_heads, key_ext, preferred_element_type=jnp.float32
    ) / math.sqrt(head_dim)
    scores = jnp.where(seen[:, None], scores, -jnp.inf)
    highest = jnp.max(scores, axis=-1, keepdims=True)
    expo = jnp.exp(scores - highest)
    probs = (expo / jnp.sum(expo, axis=-1, keepdims=True)).astype(jnp.bfloat16)
    attended = jnp.einsum("chts,cshp->cthp", probs, value_ext, preferred_element_type=jnp.float32)
    layer_out = (
        (normed + attended)
        .reshape(clip_count, row_count, head_count * head_dim)
        .astype(jnp.bfloat16)
    )
    grad_x = jnp.einsum("chts,cthp->cshp", mixing, cotan_heads, preferred_element_type=jnp.float32)
    grad_x = grad_x + tail_fall[..., None] * jnp.einsum(
        "chpn,csn->cshp", grad_in, b_wide, precision=precise
    )
    input_grad = grad_x.reshape(clip_count, row_count, head_count * head_dim).astype(jnp.bfloat16)
    product = jnp.einsum(
        "cthp,cshp->chts", cotan_heads, scan_heads, preferred_element_type=jnp.float32
    )
    weigh = (product * decay_mat * state_scale).astype(jnp.bfloat16)
    grad_b = jnp.einsum("chts,ctn->chsn", weigh, c_rows, preferred_element_type=jnp.float32)
    grad_b = grad_b + jnp.swapaxes(tail_fall, 1, 2)[..., None] * jnp.einsum(
        "cshp,chpn->chsn", scan_wide, grad_in, precision=precise
    )
    gradient_readout = jnp.einsum(
        "chts,csn->chtn", weigh, b_rows, preferred_element_type=jnp.float32
    )
    gradient_readout = gradient_readout + jnp.swapaxes(head_rise, 1, 2)[
        ..., None
    ] * state_scale * jnp.einsum("cthp,chpn->chtn", cotan_wide, state_in, precision=precise)
    both = jnp.concatenate([grad_b, gradient_readout], axis=-1).astype(jnp.bfloat16)
    share_rows = model_width // lax.axis_size("space")
    term = jnp.zeros((lax.axis_size("space") * share_rows, 2 * state_count), jnp.float32)
    for head in range(head_count):
        term = term + jnp.einsum(
            "crd,crn->dn", latents, both[:, head], preferred_element_type=jnp.float32
        )
    share = lax.psum_scatter(
        term.astype(jnp.bfloat16), "space", scatter_dimension=0, tiled=True
    ).astype(jnp.float32)
    summed = lax.psum(share, ("tm", "dp"))
    proj_grad = summed / math.sqrt(
        clip_count * lax.axis_size("dp") * row_count * lax.axis_size("tm")
    )
    return (layer_out, input_grad, proj_grad)


def solution(mesh):
    return jax.shard_map(
        on_device,
        mesh=mesh,
        in_specs=(
            P("dp", "tm", None),
            P(),
            P(),
            P("dp", "tm", "space"),
            P("dp", "tm", "space"),
            P("dp", "tm", "space"),
            P("dp", "tm", "space"),
            P("dp", "tm", "space"),
            P("dp", "tm", "space"),
            P("dp", "tm"),
        ),
        out_specs=(P("dp", "tm", "space"), P("dp", "tm", "space"), P("space", None)),
        check_vma=False,
    )
```

profile of v0, /device:TPU:0, one launch (start us, length us, event | category | flops | bytes accessed | tf_op | source)
XLA Modules:
  0.0 185.3 jit_solution(13750786870784752532)
XLA Ops:
  7.2 1.7 slice.42
  9.0 3.0 %collective-permute-start.2 = (bf16[1,128,1024]{2,1,0:T(8,128)(2,1)}, bf16[1,128,1024]{2,1,0:T(8,128)(2,1)}, u32[]{:S(2)}, u32[]{:S(2)}) collective-permute-start(bf16[1,128,1024]{2,1,0:T(8,128)(2,1)} %slice.42), channel_id=1, source_target_pairs={{0,8},{8,16},{16,24},{1,9},{9,17},{17,25},{2,10},{10,18},{18,26},{... | collective-permute-start | bytes 786440 | tf_op jit(solution)/shard_map/ppermute | solution.py:18
  14.1 4.5 %collective-permute-start.3 = (bf16[1,128,1024]{1,2,0:T(8,128)(2,1)}, bf16[1,128,1024]{1,2,0:T(8,128)(2,1)}, u32[]{:S(2)}, u32[]{:S(2)}) collective-permute-start(bf16[1,128,1024]{1,2,0:T(8,128)(2,1)} %slice.54), channel_id=1, source_target_pairs={{0,8},{8,16},{16,24},{1,9},{9,17},{17,25},{2,10},{10,18},{18,26},{... | collective-permute-start | bytes 786440 | tf_op jit(solution)/shard_map/ppermute | solution.py:18
  22.1 1.6 copy.60
  23.6 2.2 %convert_multiply_fusion.1 = f32[1,256,1024]{2,1,0:T(8,128)} fusion(f32[1,256,1024]{2,1,0:T(8,128)S(1)} %copy.60, bf16[1,256,1024]{2,1,0:T(8,128)(2,1)} %param.17), kind=kLoop, calls=%fused_computation.81 | loop fusion | flops 524288 | bytes 2621440 | tf_op jit(solution)/shard_map/mul | solution.py:69
  25.8 2.6 %copy.88 = f32[1,256,1024]{1,2,0:T(8,128)} copy(f32[1,256,1024]{2,1,0:T(8,128)} %convert_multiply_fusion.1) | data formatting | bytes 2097152 | tf_op jit(solution)/shard_map/mul | solution.py:69
  32.4 1.6 copy.69
  34.0 2.2 %convert_multiply_fusion = f32[1,256,1024]{2,1,0:T(8,128)} fusion(f32[1,256,1024]{2,1,0:T(8,128)S(1)} %copy.69, bf16[1,256,1024]{2,1,0:T(8,128)(2,1)} %param.22), kind=kLoop, calls=%fused_computation.79 | loop fusion | flops 524288 | bytes 2621440 | tf_op jit(solution)/shard_map/mul | solution.py:72
  36.2 2.6 %copy.89 = f32[1,256,1024]{1,2,0:T(8,128)} copy(f32[1,256,1024]{2,1,0:T(8,128)} %convert_multiply_fusion) | data formatting | bytes 2097152 | tf_op jit(solution)/shard_map/mul | solution.py:72
  39.4 1.8 convolution_bitcast_fusion.3
  41.3 1.8 multiply_convert_fusion
  43.1 1.4 fusion.89
  46.9 22.6 %while.23 = (s32[]{:T(128)}, f32[1,8,128,128]{3,2,1,0:T(8,128)S(1)}, f32[1,8]{1,0:T(1,128)}, f32[1,8,128,128]{3,2,1,0:T(8,128)S(1)}, s32[]{:T(128)}, /*index=5*/s32[]{:T(128)}) while((s32[]{:T(128)}, f32[1,8,128,128]{3,2,1,0:T(8,128)S(1)}, f32[1,8]{1,0:T(1,128)}, f32[1,8,128,128]{3,2,1,0:T(8,128)S(1)}, s32[]{:T(128)}, ...), condition=%wide.region_8.9_spmd.clone, body=%wide.region_7.8_spmd.clone.sunk | while | flops 655363 | bytes 3145879 | solution.py:87
  46.9 1.4 fusion.125
  49.6 2.3 %collective-permute-done.1 = bf16[1,8,128,128]{3,2,1,0:T(8,128)(2,1)S(1)} collective-permute-done((bf16[1,8,128,128]{3,2,1,0:T(8,128)(2,1)}, bf16[1,8,128,128]{3,2,1,0:T(8,128)(2,1)S(1)}, u32[]{:S(2)}, u32[]{:S(2)}) %collective-permute-start.1) | collective-permute-done | bytes 262176 | tf_op jit(solution)/shard_map/while/body/eval_jaxpr/ppermute | solution.py:18
  54.7 5.5 %collective-permute-done.1 = bf16[1,8,128,128]{3,2,1,0:T(8,128)(2,1)S(1)} collective-permute-done((bf16[1,8,128,128]{3,2,1,0:T(8,128)(2,1)}, bf16[1,8,128,128]{3,2,1,0:T(8,128)(2,1)S(1)}, u32[]{:S(2)}, u32[]{:S(2)}) %collective-permute-start.1) | collective-permute-done | bytes 262176 | tf_op jit(solution)/shard_map/while/body/eval_jaxpr/ppermute | solution.py:18
  60.2 1.4 fusion.125
  62.9 6.6 %collective-permute-done.1 = bf16[1,8,128,128]{3,2,1,0:T(8,128)(2,1)S(1)} collective-permute-done((bf16[1,8,128,128]{3,2,1,0:T(8,128)(2,1)}, bf16[1,8,128,128]{3,2,1,0:T(8,128)(2,1)S(1)}, u32[]{:S(2)}, u32[]{:S(2)}) %collective-permute-start.1) | collective-permute-done | bytes 262176 | tf_op jit(solution)/shard_map/while/body/eval_jaxpr/ppermute | solution.py:18
  69.6 2.0 %fusion.27 = bf16[1,8,256,128]{2,3,1,0:T(8,128)(2,1)S(1)} fusion(f32[8,256,128]{1,2,0:T(8,128)} %fusion.87, f32[1,8,128,128]{3,2,1,0:T(8,128)S(1)} %get-tuple-element.48, f32[8,256]{1,0:T(8,128)} %subtract_exponential_fusion.1, bf16[256,8,128]{2,1,0:T(8,128)(2,1)} %bitcast.209), kind=kOutput, calls=%fused_computation.62 | convolution fusion | flops 403439616 | bytes 2629632 | tf_op jit(solution)/shard_map/cshp,chpn->chsn/dot_general | solution.py:135
  71.6 26.0 %while.22 = (s32[]{:T(128)}, f32[1,8,128,128]{3,2,1,0:T(8,128)S(1)}, f32[1,8]{1,0:T(1,128)}, f32[1,8,128,128]{3,2,1,0:T(8,128)S(1)}, s32[]{:T(128)}, /*index=5*/s32[]{:T(128)}) while((s32[]{:T(128)}, f32[1,8,128,128]{3,2,1,0:T(8,128)S(1)}, f32[1,8]{1,0:T(1,128)}, f32[1,8,128,128]{3,2,1,0:T(8,128)S(1)}, s32[]{:T(128)}, ...), condition=%wide.region_3.4_spmd.clone, body=%wide.region_2.3_spmd.clone.sunk | while | flops 655363 | bytes 3145879 | solution.py:86
  71.6 1.4 fusion.124
  73.0 6.7 %collective-permute-start = (bf16[1,8,128,128]{3,2,1,0:T(8,128)(2,1)}, bf16[1,8,128,128]{3,2,1,0:T(8,128)(2,1)S(1)}, u32[]{:S(2)}, u32[]{:S(2)}) collective-permute-start(bf16[1,8,128,128]{3,2,1,0:T(8,128)(2,1)} %fusion.124), channel_id=1, source_target_pairs={{0,8},{8,16},{16,24},{1,9},{9,17},{17,25},{2,10},{10,18},{18,26},{... | collective-permute-start | bytes 786440 | tf_op jit(solution)/shard_map/while/body/eval_jaxpr/ppermute | solution.py:18
  81.1 1.4 fusion.124
  82.5 4.2 %collective-permute-start = (bf16[1,8,128,128]{3,2,1,0:T(8,128)(2,1)}, bf16[1,8,128,128]{3,2,1,0:T(8,128)(2,1)S(1)}, u32[]{:S(2)}, u32[]{:S(2)}) collective-permute-start(bf16[1,8,128,128]{3,2,1,0:T(8,128)(2,1)} %fusion.124), channel_id=1, source_target_pairs={{0,8},{8,16},{16,24},{1,9},{9,17},{17,25},{2,10},{10,18},{18,26},{... | collective-permute-start | bytes 786440 | tf_op jit(solution)/shard_map/while/body/eval_jaxpr/ppermute | solution.py:18
  88.0 1.4 fusion.124
  89.5 6.5 %collective-permute-start = (bf16[1,8,128,128]{3,2,1,0:T(8,128)(2,1)}, bf16[1,8,128,128]{3,2,1,0:T(8,128)(2,1)S(1)}, u32[]{:S(2)}, u32[]{:S(2)}) collective-permute-start(bf16[1,8,128,128]{3,2,1,0:T(8,128)(2,1)} %fusion.124), channel_id=1, source_target_pairs={{0,8},{8,16},{16,24},{1,9},{9,17},{17,25},{2,10},{10,18},{18,26},{... | collective-permute-start | bytes 786440 | tf_op jit(solution)/shard_map/while/body/eval_jaxpr/ppermute | solution.py:18
  97.6 2.0 %fusion.26 = bf16[1,8,256,128]{2,3,1,0:T(8,128)(2,1)S(1)} fusion(f32[8,256,128]{1,2,0:T(8,128)} %fusion.89, f32[1,8,128,128]{3,2,1,0:T(8,128)S(1)} %get-tuple-element.47, f32[8,256]{1,0:T(8,128)} %get-tuple-element.106, bf16[256,8,128]{2,1,0:T(8,128)(2,1)} %bitcast.213), kind=kOutput, calls=%fused_computation.61 | convolution fusion | flops 403439616 | bytes 2629632 | tf_op jit(solution)/shard_map/cthp,chpn->chtn/dot_general | solution.py:143
  102.9 1.4 fusion.6
  104.4 2.0 %fusion.17 = f32[1,256,8,128]{1,3,2,0:T(8,128)} fusion(f32[1,8,128,128]{3,2,1,0:T(8,128)S(1)} %get-tuple-element.47, f32[256,8]{0,1:T(8,128)S(1)} %get-tuple-element.108, bf16[256,128]{1,0:T(8,128)(2,1)S(1)} %convolution_convert_fusion.1), kind=kOutput, calls=%fused_computation.49 | convolution fusion | flops 402980864 | bytes 1646592 | tf_op jit(solution)/shard_map/ctn,chpn->cthp/dot_general | solution.py:92
  107.9 1.9 %multiply_reduce_fusion = (f32[256,8]{0,1:T(8,128)S(1)}, f32[1,256,8,128]{1,3,2,0:T(8,128)}) fusion(f32[1,256,8,128]{1,3,2,0:T(8,128)S(1)} %copy-done.10, bf16[256,8,128]{2,1,0:T(8,128)(2,1)S(1)} %bitcast.211, f32[8,256]{1,0:T(8,128)S(1)} %copy-done.18, f32[256,256]{1,0:T(8,128)S(1)} %convolution_multiply_fusion.4, pred[256,256]{1,0:T(8,128)(4,1)S(1)} %copy-done.16), kind=kOutput, calls=%fused_computation.80 | convolution fusion | flops 137099264 | bytes 2965504 | tf_op jit(solution)/shard_map/chts,cshp->cthp/dot_general | solution.py:91
  118.9 19.4 %reduce-scatter.2.cloned.1.call-done = bf16[512,256]{0,1:T(8,128)(2,1)} async-done(((bf16[2048,256]{0,1:T(8,128)(2,1)}), bf16[512,256]{0,1:T(8,128)(2,1)}) %reduce-scatter.2.cloned.1.call-update) | async-done | bytes 262160 | tf_op jit(solution)/shard_map/reduce_scatter | solution.py:151
  138.3 39.1 %all-reduce.1 = f32[512,256]{0,1:T(8,128)S(1)} all-reduce(bf16[512,256]{0,1:T(8,128)(2,1)} %reduce-scatter.2.cloned.1.call-done), channel_id=1, replica_groups=mesh['tm'=4,'space'=4,'dp'=2] {'tm','dp'}, use_global_device_ids=true, to_apply=%region_10.11 | all-reduce | flops 131072 | bytes 786432 | tf_op jit(solution)/shard_map/psum | solution.py:154
  (109 shorter events, 36.8 us)
Async XLA Ops:
  7.2 21.3 %copy-start = (bf16[1,256,2048]{2,1,0:T(8,128)(2,1)S(1)}, bf16[1,256,2048]{2,1,0:T(8,128)(2,1)}, u32[]{:S(2)}) copy-start(bf16[1,256,2048]{2,1,0:T(8,128)(2,1)} %param.14) | copy-start | bytes 3145732
  7.2 11.5 %copy-start.19 = (f32[1,256,8]{1,2,0:T(8,128)S(1)}, f32[1,256,8]{1,2,0:T(8,128)}, u32[]{:S(2)}) copy-start(f32[1,256,8]{1,2,0:T(8,128)} %param.18) | copy-start | bytes 24580
  7.2 131.1 %reduce-scatter.2.cloned.1.call-start = ((), (), s32[]{:S(2)}) async-start(), calls=%async_computation.1 | async-start | bytes 1310720 | tf_op jit(solution)/shard_map/reduce_scatter | solution.py:151
  9.0 103.0 %collective-permute-start.2 = (bf16[1,128,1024]{2,1,0:T(8,128)(2,1)}, bf16[1,128,1024]{2,1,0:T(8,128)(2,1)}, u32[]{:S(2)}, u32[]{:S(2)}) collective-permute-start(bf16[1,128,1024]{2,1,0:T(8,128)(2,1)} %slice.42), channel_id=1, source_target_pairs={{0,8},{8,16},{16,24},{1,9},{9,17},{17,25},{2,10},{10,18},{18,26},{... | collective-permute-start | bytes 786440 | tf_op jit(solution)/shard_map/ppermute | solution.py:18
  13.3 0.9 copy-start.2
  14.1 100.0 %collective-permute-start.3 = (bf16[1,128,1024]{1,2,0:T(8,128)(2,1)}, bf16[1,128,1024]{1,2,0:T(8,128)(2,1)}, u32[]{:S(2)}, u32[]{:S(2)}) collective-permute-start(bf16[1,128,1024]{1,2,0:T(8,128)(2,1)} %slice.54), channel_id=1, source_target_pairs={{0,8},{8,16},{16,24},{1,9},{9,17},{17,25},{2,10},{10,18},{18,26},{... | collective-permute-start | bytes 786440 | tf_op jit(solution)/shard_map/ppermute | solution.py:18
  20.2 21.1 %copy-start.17 = (f32[8,256]{1,0:T(8,128)}, f32[8,256]{1,0:T(8,128)S(1)}, u32[]{:S(2)}) copy-start(f32[8,256]{1,0:T(8,128)S(1)} %get-tuple-element.107) | copy-start | bytes 24580
  20.2 21.0 %copy-start.15 = (pred[256,256]{1,0:T(8,128)(4,1)}, pred[256,256]{1,0:T(8,128)(4,1)S(1)}, u32[]{:S(2)}) copy-start(pred[256,256]{1,0:T(8,128)(4,1)S(1)} %iota_compare_fusion) | copy-start | bytes 196612
  25.8 2.6 %copy-start.12 = (bf16[2048,128]{1,0:T(8,128)(2,1)S(1)}, bf16[2048,128]{1,0:T(8,128)(2,1)}, u32[]{:S(2)}) copy-start(bf16[2048,128]{1,0:T(8,128)(2,1)} %param.15) | copy-start | bytes 1572868
  25.8 3.1 %copy-start.13 = (bf16[2048,128]{1,0:T(8,128)(2,1)S(1)}, bf16[2048,128]{1,0:T(8,128)(2,1)}, u32[]{:S(2)}) copy-start(bf16[2048,128]{1,0:T(8,128)(2,1)} %param.16) | copy-start | bytes 1572868
  28.5 1.0 copy-start.4
  28.5 1.9 %copy-start.5 = (bf16[1,256,1024]{2,1,0:T(8,128)(2,1)S(1)}, bf16[1,256,1024]{2,1,0:T(8,128)(2,1)}, u32[]{:S(2)}) copy-start(bf16[1,256,1024]{2,1,0:T(8,128)(2,1)} %param.22) | copy-start | bytes 1572868
  36.2 5.1 %copy-start.6 = (bf16[32,8,8,128]{3,2,1,0:T(8,128)(2,1)S(1)}, bf16[32,8,8,128]{3,2,1,0:T(8,128)(2,1)}, u32[]{:S(2)}) copy-start(bf16[32,8,8,128]{3,2,1,0:T(8,128)(2,1)} %copy.92) | copy-start | bytes 1572868
  43.1 2.8 %copy-start.1 = (f32[1,256,1024]{1,2,0:T(8,128)S(1)}, f32[1,256,1024]{1,2,0:T(8,128)}, u32[]{:S(2)}) copy-start(f32[1,256,1024]{1,2,0:T(8,128)} %copy.89) | copy-start | bytes 3145732
  48.3 3.6 %collective-permute-start.1 = (bf16[1,8,128,128]{3,2,1,0:T(8,128)(2,1)}, bf16[1,8,128,128]{3,2,1,0:T(8,128)(2,1)S(1)}, u32[]{:S(2)}, u32[]{:S(2)}) collective-permute-start(bf16[1,8,128,128]{3,2,1,0:T(8,128)(2,1)} %fusion.125), channel_id=1, source_target_pairs={{8,0},{16,8},{24,16},{9,1},{17,9},{25,17},{10,2},{18,10},{26,18},{... | collective-permute-start | bytes 786440 | tf_op jit(solution)/shard_map/while/body/eval_jaxpr/ppermute | solution.py:18
  53.4 6.8 %collective-permute-start.1 = (bf16[1,8,128,128]{3,2,1,0:T(8,128)(2,1)}, bf16[1,8,128,128]{3,2,1,0:T(8,128)(2,1)S(1)}, u32[]{:S(2)}, u32[]{:S(2)}) collective-permute-start(bf16[1,8,128,128]{3,2,1,0:T(8,128)(2,1)} %fusion.125), channel_id=1, source_target_pairs={{8,0},{16,8},{24,16},{9,1},{17,9},{25,17},{10,2},{18,10},{26,18},{... | collective-permute-start | bytes 786440 | tf_op jit(solution)/shard_map/while/body/eval_jaxpr/ppermute | solution.py:18
  61.6 7.9 %collective-permute-start.1 = (bf16[1,8,128,128]{3,2,1,0:T(8,128)(2,1)}, bf16[1,8,128,128]{3,2,1,0:T(8,128)(2,1)S(1)}, u32[]{:S(2)}, u32[]{:S(2)}) collective-permute-start(bf16[1,8,128,128]{3,2,1,0:T(8,128)(2,1)} %fusion.125), channel_id=1, source_target_pairs={{8,0},{16,8},{24,16},{9,1},{17,9},{25,17},{10,2},{18,10},{26,18},{... | collective-permute-start | bytes 786440 | tf_op jit(solution)/shard_map/while/body/eval_jaxpr/ppermute | solution.py:18
  73.0 8.0 %collective-permute-start = (bf16[1,8,128,128]{3,2,1,0:T(8,128)(2,1)}, bf16[1,8,128,128]{3,2,1,0:T(8,128)(2,1)S(1)}, u32[]{:S(2)}, u32[]{:S(2)}) collective-permute-start(bf16[1,8,128,128]{3,2,1,0:T(8,128)(2,1)} %fusion.124), channel_id=1, source_target_pairs={{0,8},{8,16},{16,24},{1,9},{9,17},{17,25},{2,10},{10,18},{18,26},{... | collective-permute-start | bytes 786440 | tf_op jit(solution)/shard_map/while/body/eval_jaxpr/ppermute | solution.py:18
  82.5 5.5 %collective-permute-start = (bf16[1,8,128,128]{3,2,1,0:T(8,128)(2,1)}, bf16[1,8,128,128]{3,2,1,0:T(8,128)(2,1)S(1)}, u32[]{:S(2)}, u32[]{:S(2)}) collective-permute-start(bf16[1,8,128,128]{3,2,1,0:T(8,128)(2,1)} %fusion.124), channel_id=1, source_target_pairs={{0,8},{8,16},{16,24},{1,9},{9,17},{17,25},{2,10},{10,18},{18,26},{... | collective-permute-start | bytes 786440 | tf_op jit(solution)/shard_map/while/body/eval_jaxpr/ppermute | solution.py:18
  89.5 7.9 %collective-permute-start = (bf16[1,8,128,128]{3,2,1,0:T(8,128)(2,1)}, bf16[1,8,128,128]{3,2,1,0:T(8,128)(2,1)S(1)}, u32[]{:S(2)}, u32[]{:S(2)}) collective-permute-start(bf16[1,8,128,128]{3,2,1,0:T(8,128)(2,1)} %fusion.124), channel_id=1, source_target_pairs={{0,8},{8,16},{16,24},{1,9},{9,17},{17,25},{2,10},{10,18},{18,26},{... | collective-permute-start | bytes 786440 | tf_op jit(solution)/shard_map/while/body/eval_jaxpr/ppermute | solution.py:18
  104.3 2.3 %copy-start.20 = (s32[1,2]{1,0:T(1,128)S(1)}, s32[1,2]{1,0:T(1,128)}, u32[]{:S(2)}) copy-start(s32[1,2]{1,0:T(1,128)} %param.23) | copy-start | bytes 28
  104.3 2.4 %copy-start.8 = (bf16[32,8,8,128]{3,2,1,0:T(8,128)(2,1)S(1)}, bf16[32,8,8,128]{3,2,1,0:T(8,128)(2,1)}, u32[]{:S(2)}) copy-start(bf16[32,8,8,128]{3,2,1,0:T(8,128)(2,1)} %copy.94) | copy-start | bytes 1572868
  104.3 2.4 %copy-start.16 = (pred[256,256]{1,0:T(8,128)(4,1)S(1)}, pred[256,256]{1,0:T(8,128)(4,1)}, u32[]{:S(2)}) copy-start(pred[256,256]{1,0:T(8,128)(4,1)} %copy-done.15) | copy-start | bytes 196612
  104.3 2.4 %copy-start.18 = (f32[8,256]{1,0:T(8,128)S(1)}, f32[8,256]{1,0:T(8,128)}, u32[]{:S(2)}) copy-start(f32[8,256]{1,0:T(8,128)} %copy-done.17) | copy-start | bytes 24580
  106.4 1.1 copy-start.7
  106.7 1.3 copy-start.10
  109.8 1.0 copy-start.14
  109.8 2.2 %copy-start.9 = (bf16[1,256,1024]{2,1,0:T(8,128)(2,1)S(1)}, bf16[1,256,1024]{2,1,0:T(8,128)(2,1)}, u32[]{:S(2)}) copy-start(bf16[1,256,1024]{2,1,0:T(8,128)(2,1)} %param.21) | copy-start | bytes 1572868
  111.0 3.2 %copy-start.3 = (bf16[1,256,1024]{1,2,0:T(8,128)(2,1)S(1)}, bf16[1,256,1024]{1,2,0:T(8,128)(2,1)}, u32[]{:S(2)}) copy-start(bf16[1,256,1024]{1,2,0:T(8,128)(2,1)} %copy-done.2) | copy-start | bytes 1572868
  115.8 1.1 copy-start.11
  115.8 1.6 copy-start.21
Sparse Core Ops, SparseCore 0:
  104.5 33.7 reduce-scatter.1
where the time goes:
time: 186 us; the launch traced here: 185 us
  blocking collectives  39.1 us (21%)
  waiting for transfers between devices  37.8 us (20%)
  starting transfers between devices  28.8 us (15%)
  matrix products  23.5 us (13%)
  local copies, waits for them, and re-layouts  22.7 us (12%)
  other arithmetic  18.6 us (10%)
  between operations  14.4 us (8%)
    psum x1, blocking collectives, on_device(): summed = lax.psum(share, ('tm', 'dp'))  39.1 us
    ppermute x8, starting transfers between devices, shifted(): return lax.ppermute(block, axis, route)  28.8 us
    reduce_scatter x1, waiting for transfers between devices, on_device(): lax.psum_scatter(term.astype(jnp.bfloat16), 'space', scatter_dimension=0,...  19.4 us
    ppermute x8, waiting for transfers between devices, shifted(): return lax.ppermute(block, axis, route)  18.4 us
    unnamed x51, local copies, waits for them, and re-layouts  7.68 us
    mul x3, local copies, waits for them, and re-layouts, on_device(): scan_wide * tail_fall[..., None]  5.22 us
    dot_general x8, matrix products, on_device(): jnp.einsum('crd,crn->dn', latents, both[:, head], preferred_element_type=...  4.72 us
    convert_element_type x3, other arithmetic, forward_step(): (carried[..., None, None] * state + fresh).astype(jnp.bfloat16)  4.22 us
  transfers between devices with their start and end apart: 9, of which 7 were waited for; matrix products, arithmetic and copies ran while one was open for 33% of the time, Pallas kernels for 0%

commit v1 on v0

v1 whole, which is shorter than its diff:
```python
import functools
import math

import jax
import jax.numpy as jnp
from jax import lax
from jax.experimental import pallas as pl
from jax.experimental.pallas import tpu as pltpu
from jax.sharding import PartitionSpec as P

W = 128
QB = 128
MESH = pl.DeviceIdType.MESH
BF = jnp.bfloat16
F32 = jnp.float32
HI = lax.Precision.HIGHEST


def mm(a, b, ca=1, cb=0, precision=None):
    return lax.dot_general(
        a, b, (((ca,), (cb,)), ((), ())), preferred_element_type=F32, precision=precision
    )


def kernel(
    sizes,
    lat_h, pi_h, po_h, x_h, ld_ref, q_h, k_h, v_h, g_h, off_ref,
    lo_h, ig_h, pg_h,
    lat, pi, po, x, g, q, kx, vx, lo, ig, pg,
    cumb, cumt, b_s, c_s, cs_s, kern, wsum, xw, rg, inner, gx, att,
    f_fresh, f_in, f_out, r_fresh, r_in, r_out,
    both, rz, zfull, term, rs, agf,
    load_sem, store_sem, chain_send, chain_recv, halo_send, halo_recv,
    zs_send, zs_recv, zg_send, zg_recv, rs_send, rs_recv, ag_send, ag_recv,
):
    n_tm, n_z, n_dp = sizes
    rows, width = x.shape
    heads = ld_ref.shape[1]
    dim = width // heads
    states = pi.shape[1]
    scale = 1.0 / math.sqrt(states)
    group = n_tm * n_dp
    share = lat.shape[1] // n_z
    owners = min(group, share // 16)
    chunk = share // owners
    zrows = rows // n_z
    tm = lax.axis_index("tm")
    z = lax.axis_index("space")
    dp = lax.axis_index("dp")
    me = dp * n_tm + tm

    def member(k):
        other = lax.rem(me + k, group)
        return other, {"dp": other // n_tm, "tm": lax.rem(other, n_tm)}

    def zmember(k):
        other = lax.rem(z + k, n_z)
        return other, {"space": other}

    loads = [
        pltpu.make_async_copy(src, dst, load_sem.at[i])
        for i, (src, dst) in enumerate(
            [
                (lat_h, lat), (pi_h, pi), (po_h, po), (x_h, x), (g_h, g),
                (k_h, kx.at[pl.ds(W, rows)]), (v_h, vx.at[pl.ds(W, rows)]), (q_h, q),
            ]
        )
    ]
    for load in loads:
        load.start()

    barrier = pltpu.get_barrier_semaphore()
    for k in range(1, group):
        pl.semaphore_signal(barrier, inc=1, device_id=member(k)[1], device_id_type=MESH)
    for k in range(1, n_z):
        pl.semaphore_signal(barrier, inc=1, device_id=zmember(k)[1], device_id_type=MESH)

    row_i = lax.broadcasted_iota(jnp.int32, (rows, rows), 0)
    col_i = lax.broadcasted_iota(jnp.int32, (rows, rows), 1)
    lower = (row_i >= col_i).astype(F32)
    ld = ld_ref[...]
    cum = mm(lower, ld, precision=HI)
    cumt[...] = mm(ld, lower, 0, 1, precision=HI)
    spread = (
        lax.broadcasted_iota(jnp.int32, (heads, width), 1) // dim
        == lax.broadcasted_iota(jnp.int32, (heads, width), 0)
    ).astype(F32)
    cumb[...] = mm(cum, spread, precision=HI)

    for load in loads[:3]:
        load.wait()
    b_s[...] = mm(lat[...], pi[...]).astype(BF)
    cf = mm(lat[...], po[...]).astype(BF)
    c_s[...] = cf
    cs_s[...] = (cf.astype(F32) * scale).astype(BF)
    kern[...] = mm(cf, b_s[...], 1, 1) * scale

    for load in loads[3:5]:
        load.wait()
    total = cumb[rows - 1 : rows, :]
    rg[...] = (jnp.exp(cumb[...]) * g[...].astype(F32)).astype(BF)
    xw[...] = (jnp.exp(total - cumb[...]) * x[...].astype(F32)).astype(BF)
    f_fresh[...] = mm(b_s[...], xw[...], 0, 0)
    r_fresh[...] = mm(cs_s[...], rg[...], 0, 0)
    pl.semaphore_wait(barrier, group - 1 + n_z - 1)

    def chain(i, fresh, src, dst, to):
        return pltpu.make_async_remote_copy(
            src_ref=src, dst_ref=dst, send_sem=chain_send.at[i], recv_sem=chain_recv.at[i],
            device_id={"tm": to}, device_id_type=MESH,
        )

    up = lax.rem(tm + 1, n_tm)
    down = lax.rem(tm + n_tm - 1, n_tm)
    fwd = chain(0, f_fresh, f_out, f_in, up)
    rev = chain(1, r_fresh, r_out, r_in, down)

    def chain_step(copy, place, fresh, src, dst):
        @pl.when(place == 0)
        def _():
            dst[...] = jnp.zeros_like(dst)

        @pl.when(place > 0)
        def _():
            copy.wait_recv()

        @pl.when(place < n_tm - 1)
        def _():
            carried = jnp.exp(cumb[rows - 1 : rows, :])
            src[...] = (carried * dst[...].astype(F32) + fresh[...]).astype(BF)
            copy.start()

    rplace = n_tm - 1 - tm
    fslot = jnp.where(tm < 2, tm, 2 * tm - 1)
    rslot = jnp.where(rplace < 2, rplace, 2 * rplace - 1)

    halos = [
        pltpu.make_async_remote_copy(
            src_ref=buf.at[pl.ds(rows, W)], dst_ref=buf.at[pl.ds(0, W)],
            send_sem=halo_send.at[i], recv_sem=halo_recv.at[i],
            device_id={"tm": up}, device_id_type=MESH,
        )
        for i, buf in enumerate((kx, vx))
    ]
    per = 2 if heads % 2 == 0 else 1
    steps = heads // per
    wsum[...] = jnp.zeros_like(wsum)
    for load in loads[5:]:
        load.wait()

    def lanes(h):
        return pl.ds(pl.multiple_of(h * dim, dim), dim)

    def local_step(i, _):
        @pl.when(fslot == i)
        def _():
            chain_step(fwd, tm, f_fresh, f_out, f_in)

        @pl.when(rslot == i)
        def _():
            chain_step(rev, rplace, r_fresh, r_out, r_in)

        @pl.when((tm < n_tm - 1) & (i == min(1, steps - 1)))
        def _():
            for halo in halos:
                halo.start()

        acc = wsum[...]
        for j in range(per):
            h = i * per + j
            at = lanes(h)
            cb = cumb[:, at]
            gap = jnp.concatenate([cb] * (rows // dim), axis=1) - cumt[pl.ds(h, 1), :]
            decay = jnp.exp(jnp.where(row_i >= col_i, gap, -jnp.inf))
            mixing = (kern[...] * decay).astype(BF)
            xh, gh = x[:, at], g[:, at]
            acc = acc + mm(gh, xh, 1, 1) * decay
            inner[:, at] = mm(mixing, xh)
            gx[:, at] = mm(mixing, gh, 0, 0)
        wsum[...] = acc
        return 0

    lax.fori_loop(0, steps, local_step, 0)

    @pl.when(fslot >= steps)
    def _():
        chain_step(fwd, tm, f_fresh, f_out, f_in)

    @pl.when(rslot >= steps)
    def _():
        chain_step(rev, rplace, r_fresh, r_out, r_in)

    weigh = (wsum[...] * scale).astype(BF)
    both[:, :states] = (mm(weigh, c_s[...], 0, 0) + mm(xw[...], r_in[...], 1, 1)).astype(BF)
    both[:, states:] = (
        mm(weigh, b_s[...]) + mm(rg[...], f_in[...], 1, 1) * scale
    ).astype(BF)
    zscatter = []
    for k in range(1, n_z):
        other, to = zmember(k)
        zscatter.append(
            pltpu.make_async_remote_copy(
                src_ref=both.at[pl.ds(pl.multiple_of(other * zrows, zrows), zrows)],
                dst_ref=rz.at[k - 1], send_sem=zs_send.at[k - 1], recv_sem=zs_recv.at[k - 1],
                device_id=to, device_id_type=MESH,
            )
        )
        zscatter[-1].start()

    a_row = lax.broadcasted_iota(jnp.int32, (QB, W + QB), 0)
    a_col = lax.broadcasted_iota(jnp.int32, (QB, W + QB), 1)

    def attend(blk):
        seen = (a_col <= a_row + W) & (a_col >= a_row + 1 + off_ref[0, blk])
        seen = seen & (a_col >= W - (tm * rows + blk * QB))

        def step(i, _):
            for j in range(per):
                at = lanes(i * per + j)
                s = mm(q[blk * QB : (blk + 1) * QB, at], kx[blk * QB : blk * QB + W + QB, at], 1, 1)
                s = jnp.where(seen, s, -jnp.inf)
                top = jnp.max(s, axis=1, keepdims=True)
                e = jnp.exp((s - top) * (1.0 / math.sqrt(dim)))
                whole = jnp.sum(e, axis=1, keepdims=True)
                o = mm(e.astype(BF), vx[blk * QB : blk * QB + W + QB, at])
                att[blk * QB : (blk + 1) * QB, at] = o / whole
            return 0

        lax.fori_loop(0, steps, step, 0)

    for blk in range(1, rows // QB):
        attend(blk)

    mine = pl.ds(pl.multiple_of(z * zrows, zrows), zrows)
    for copy in zscatter:
        copy.wait_recv()
    part = both[mine, :].astype(F32)
    for k in range(n_z - 1):
        part = part + rz[k].astype(F32)
    zfull[mine, :] = part.astype(BF)
    zgather = []
    for k in range(1, n_z):
        other, to = zmember(k)
        zgather.append(
            pltpu.make_async_remote_copy(
                src_ref=zfull.at[mine], dst_ref=zfull.at[mine],
                send_sem=zg_send.at[k - 1], recv_sem=zg_recv.at[k - 1],
                device_id=to, device_id_type=MESH,
            )
        )
        zgather[-1].start()

    @pl.when(tm > 0)
    def _():
        for halo in halos:
            halo.wait_recv()

    @pl.when(tm == 0)
    def _():
        for buf in (kx, vx):
            buf[0:W, :] = jnp.zeros((W, width), BF)

    attend(0)

    for copy in zgather:
        copy.wait_recv()
    cols = pl.ds(pl.multiple_of(z * share, share), share)
    grad = mm(lat[:, cols], zfull[...], 0, 0) * (1.0 / math.sqrt(n_dp * rows * n_tm))
    term[...] = grad.astype(BF)
    scatter = []
    for k in range(1, group):
        other, to = member(k)
        at = jnp.where(other < owners, other, 0) if owners < group else other
        copy = pltpu.make_async_remote_copy(
            src_ref=term.at[pl.ds(pl.multiple_of(at * chunk, chunk), chunk)],
            dst_ref=rs.at[k - 1], send_sem=rs_send.at[k - 1], recv_sem=rs_recv.at[k - 1],
            device_id=to, device_id_type=MESH,
        )
        scatter.append((other < owners, copy))

    def when(cond, action):
        if owners == group:
            action()
        else:
            pl.when(cond)(action)

    for cond, copy in scatter:
        when(cond, copy.start)

    def finish(i, _):
        for j in range(per):
            at = lanes(i * per + j)
            cb = cumb[:, at]
            out = inner[:, at] + jnp.exp(cb) * mm(cs_s[...], f_in[:, at])
            mean = jnp.mean(out * out, axis=1, keepdims=True)
            lo[:, at] = (out * lax.rsqrt(mean + 1e-05) + att[:, at]).astype(BF)
            fall = jnp.exp(cb[rows - 1 : rows, :] - cb)
            ig[:, at] = (gx[:, at] + fall * mm(b_s[...], r_in[:, at])).astype(BF)
        return 0

    lax.fori_loop(0, steps, finish, 0)
    stores = [
        pltpu.make_async_copy(src, dst, store_sem.at[i])
        for i, (src, dst) in enumerate([(lo, lo_h), (ig, ig_h), (pg, pg_h)])
    ]
    stores[0].start()
    stores[1].start()

    own = jnp.where(me < owners, me, 0) if owners < group else me
    owned = pl.ds(pl.multiple_of(own * chunk, chunk), chunk)
    gather = []
    for k in range(1, group):
        other, to = member(k)
        copy = pltpu.make_async_remote_copy(
            src_ref=agf.at[owned], dst_ref=agf.at[owned],
            send_sem=ag_send.at[k - 1], recv_sem=ag_recv.at[k - 1],
            device_id=to, device_id_type=MESH,
        )
        gather.append((lax.rem(me + group - k, group) < owners, copy))

    def own_sum():
        for _, copy in scatter:
            copy.wait_recv()
        part = term[owned, :].astype(F32)
        for k in range(group - 1):
            part = part + rs[k].astype(F32)
        agf[owned, :] = part.astype(BF)
        for _, copy in gather:
            copy.start()

    when(me < owners, own_sum)
    for cond, copy in gather:
        when(cond, copy.wait_recv)
    pg[...] = agf[...].astype(F32)
    stores[2].start()

    for copy in zscatter + zgather:
        copy.wait_send()
    for cond, copy in scatter:
        when(cond, copy.wait_send)

    def gathered():
        for _, copy in gather:
            copy.wait_send()

    when(me < owners, gathered)

    @pl.when(tm < n_tm - 1)
    def _():
        fwd.wait_send()
        for halo in halos:
            halo.wait_send()

    @pl.when(tm > 0)
    def _():
        rev.wait_send()

    for store in stores:
        store.wait()


def on_device(
    sizes,
    latents,
    proj_input,
    proj_output,
    scan_input,
    log_decay,
    att_queries,
    att_keys,
    att_values,
    scan_cotangent,
    window_offsets,
):
    n_tm, n_z, n_dp = sizes
    clips, rows, model = latents.shape
    assert clips == 1
    width = scan_input.shape[2]
    heads = log_decay.shape[2]
    states = proj_input.shape[1]
    share = model // n_z
    group = n_tm * n_dp
    owners = min(group, share // 16)
    chunk = share // owners
    zrows = rows // n_z
    hbm = pl.BlockSpec(memory_space=pl.ANY)
    vmem = pl.BlockSpec(memory_space=pltpu.VMEM)
    smem = pl.BlockSpec(memory_space=pltpu.SMEM)

    def v(shape, kind=BF):
        return pltpu.VMEM(shape, kind)

    dma = pltpu.SemaphoreType.DMA
    layer_out, input_grad, proj_grad = pl.pallas_call(
        functools.partial(kernel, sizes),
        out_shape=(
            jax.ShapeDtypeStruct((rows, width), BF),
            jax.ShapeDtypeStruct((rows, width), BF),
            jax.ShapeDtypeStruct((share, 2 * states), F32),
        ),
        in_specs=[hbm, hbm, hbm, hbm, vmem, hbm, hbm, hbm, hbm, smem],
        out_specs=(hbm, hbm, hbm),
        scratch_shapes=[
            v((rows, model)), v((model, states)), v((model, states)),
            v((rows, width)), v((rows, width)), v((rows, width)),
            v((W + rows, width)), v((W + rows, width)),
            v((rows, width)), v((rows, width)), v((share, 2 * states), F32),
            v((rows, width), F32), v((heads, rows), F32),
            v((rows, states)), v((rows, states)), v((rows, states)),
            v((rows, rows), F32), v((rows, rows), F32),
            v((rows, width)), v((rows, width)),
            v((rows, width), F32), v((rows, width), F32), v((rows, width), F32),
            v((states, width), F32), v((states, width)), v((states, width)),
            v((states, width), F32), v((states, width)), v((states, width)),
            v((rows, 2 * states)), v((n_z - 1, zrows, 2 * states)), v((rows, 2 * states)),
            v((share, 2 * states)), v((group - 1, chunk, 2 * states)), v((share, 2 * states)),
            dma((8,)), dma((3,)), dma((2,)), dma((2,)), dma((2,)), dma((2,)),
            dma((n_z - 1,)), dma((n_z - 1,)), dma((n_z - 1,)), dma((n_z - 1,)),
            dma((group - 1,)), dma((group - 1,)), dma((group - 1,)), dma((group - 1,)),
        ],
        compiler_params=pltpu.CompilerParams(
            collective_id=0, has_side_effects=True, vmem_limit_bytes=48 * 1024 * 1024
        ),
    )(
        latents[0], proj_input, proj_output, scan_input[0], log_decay[0],
        att_queries[0], att_keys[0], att_values[0], scan_cotangent[0], window_offsets,
    )
    return layer_out[None], input_grad[None], proj_grad


def solution(mesh):
    sizes = (mesh.shape["tm"], mesh.shape["space"], mesh.shape["dp"])
    return jax.shard_map(
        functools.partial(on_device, sizes),
        mesh=mesh,
        in_specs=(
            P("dp", "tm", None),
            P(),
            P(),
            P("dp", "tm", "space"),
            P("dp", "tm", "space"),
            P("dp", "tm", "space"),
            P("dp", "tm", "space"),
            P("dp", "tm", "space"),
            P("dp", "tm", "space"),
            P("dp", "tm"),
        ),
        out_specs=(P("dp", "tm", "space"), P("dp", "tm", "space"), P("space", None)),
        check_vma=False,
    )
```

time: 186 us -> 45.2 us (0.24)
  blocking collectives: 39.1 us -> 0 us
  waiting for transfers between devices: 37.8 us -> 0 us
  Pallas kernels: 0 us -> 32.9 us
  starting transfers between devices: 28.8 us -> 0 us
  matrix products: 23.5 us -> 0 us
  other arithmetic: 18.6 us -> 0 us
  between operations: 14.4 us -> 0.67 us
  local copies, waits for them, and re-layouts: 22.7 us -> 11.1 us
    psum x1 -> x0, blocking collectives: 39.1 us -> none  [on_device(): summed = lax.psum(share, ('tm', 'dp'))]
    pallas_call x0 -> x1, Pallas kernels: none -> 32.9 us  [on_device(): pl.pallas_call(functools.partial(kernel, sizes), out_shape=(jax.ShapeDtyp...]
    ppermute x8 -> x0, starting transfers between devices: 28.8 us -> none  [shifted(): return lax.ppermute(block, axis, route)]
    dot_general x24 -> x0, matrix products: 23.5 us -> none  [the longest x8 4.72 us: on_device(): jnp.einsum('crd,crn->dn', latents, both[:, head], preferred_element_type=...]
    reduce_scatter x1 -> x0, waiting for transfers between devices: 19.4 us -> none  [on_device(): lax.psum_scatter(term.astype(jnp.bfloat16), 'space', scatter_dimension=0,...]
    ppermute x8 -> x0, waiting for transfers between devices: 18.4 us -> none  [shifted(): return lax.ppermute(block, axis, route)]
    mul x6 -> x0, local copies, waits for them, and re-layouts: 10.5 us -> none  [the longest x3 5.22 us: on_device(): scan_wide * tail_fall[..., None]]
    convert_element_type x12 -> x0, other arithmetic: 8.63 us -> none  [the longest x3 4.22 us: forward_step(): (carried[..., None, None] * state + fresh).astype(jnp.bfloat16)]
  transfers between devices with their start and end apart: 9 -> 0, of which waited for: 7 -> 0; matrix products, arithmetic and copies ran while one was open for 33% -> 0% of each run, Pallas kernels for 0% -> 0%
where the time goes in v1:
time: 45.2 us; the launch traced here: 44.7 us
  Pallas kernels  32.9 us (73%)
  local copies, waits for them, and re-layouts  11.1 us (25%)
  between operations  0.67 us (1%)
    pallas_call x1, Pallas kernels, on_device(): pl.pallas_call(functools.partial(kernel, sizes), out_shape=(jax.ShapeDtyp...  32.9 us
    unnamed x22, local copies, waits for them, and re-layouts  11.1 us

profile of v1, /device:TPU:0, one launch (start us, length us, event | category | flops | bytes accessed | tf_op | source)
XLA Modules:
  0.0 44.7 jit_solution(5322049197281075254)
XLA Ops:
  0.6 0.0 copy-start.8
  0.6 0.7 %copy-done.8 = f32[1,256,8]{1,2,0:T(8,128)S(1)} copy-done((f32[1,256,8]{1,2,0:T(8,128)S(1)}, f32[1,256,8]{1,2,0:T(8,128)}, u32[]{:S(2)}) %copy-start.8) | copy-done | bytes 8216
  1.3 0.1 copy.13
  1.5 0.0 copy-start.7
  1.5 0.7 %copy-done.7 = s32[1,2]{1,0:T(1,128)S(1)} copy-done((s32[1,2]{1,0:T(1,128)S(1)}, s32[1,2]{1,0:T(1,128)}, u32[]{:S(2)}) %copy-start.7) | copy-done | bytes 32
  2.1 0.0 copy-start
  2.1 1.0 %copy-done = bf16[2048,128]{1,0:T(8,128)(2,1)S(1)} copy-done((bf16[2048,128]{1,0:T(8,128)(2,1)S(1)}, bf16[2048,128]{1,0:T(8,128)(2,1)}, u32[]{:S(2)}) %copy-start) | copy-done | bytes 524312
  3.2 0.0 copy-start.1
  3.2 1.0 %copy-done.1 = bf16[2048,128]{1,0:T(8,128)(2,1)S(1)} copy-done((bf16[2048,128]{1,0:T(8,128)(2,1)S(1)}, bf16[2048,128]{1,0:T(8,128)(2,1)}, u32[]{:S(2)}) %copy-start.1) | copy-done | bytes 524312
  4.2 0.0 copy-start.2
  4.2 1.0 %copy-done.2 = bf16[1,256,1024]{2,1,0:T(8,128)(2,1)S(1)} copy-done((bf16[1,256,1024]{2,1,0:T(8,128)(2,1)S(1)}, bf16[1,256,1024]{2,1,0:T(8,128)(2,1)}, u32[]{:S(2)}) %copy-start.2) | copy-done | bytes 524312
  5.2 0.0 copy-start.3
  5.2 1.0 %copy-done.3 = bf16[1,256,1024]{2,1,0:T(8,128)(2,1)S(1)} copy-done((bf16[1,256,1024]{2,1,0:T(8,128)(2,1)S(1)}, bf16[1,256,1024]{2,1,0:T(8,128)(2,1)}, u32[]{:S(2)}) %copy-start.3) | copy-done | bytes 524312
  6.3 0.0 copy-start.4
  6.3 1.0 %copy-done.4 = bf16[1,256,1024]{2,1,0:T(8,128)(2,1)S(1)} copy-done((bf16[1,256,1024]{2,1,0:T(8,128)(2,1)S(1)}, bf16[1,256,1024]{2,1,0:T(8,128)(2,1)}, u32[]{:S(2)}) %copy-start.4) | copy-done | bytes 524312
  7.3 0.0 copy-start.5
  7.3 1.0 %copy-done.5 = bf16[1,256,1024]{2,1,0:T(8,128)(2,1)S(1)} copy-done((bf16[1,256,1024]{2,1,0:T(8,128)(2,1)S(1)}, bf16[1,256,1024]{2,1,0:T(8,128)(2,1)}, u32[]{:S(2)}) %copy-start.5) | copy-done | bytes 524312
  8.4 0.0 copy-start.6
  8.4 1.0 %copy-done.6 = bf16[1,256,1024]{2,1,0:T(8,128)(2,1)S(1)} copy-done((bf16[1,256,1024]{2,1,0:T(8,128)(2,1)S(1)}, bf16[1,256,1024]{2,1,0:T(8,128)(2,1)}, u32[]{:S(2)}) %copy-start.6) | copy-done | bytes 524312
  9.4 32.9 %shard_map.121 = (bf16[256,1024]{1,0:T(8,128)(2,1)S(1)}, bf16[256,1024]{1,0:T(8,128)(2,1)S(1)}, f32[512,256]{1,0:T(8,128)S(1)}) custom-call(bf16[256,2048]{1,0:T(8,128)(2,1)} %bitcast.17, bf16[2048,128]{1,0:T(8,128)(2,1)S(1)} %copy-done, bf16[2048,128]{1,0:T(8,128)(2,1)S(1)} %copy-done.1, bf16[256,1024]{1,0:T(8,128)(2,1)S(1)} %bitcast.9, ...), custom_call_target="tpu_custom_call" | custom-call | tf_op jit(solution)/shard_map/pallas_call | solution.py:394
  42.3 0.8 %copy.17 = bf16[1,256,1024]{2,1,0:T(8,128)(2,1)} copy(bf16[1,256,1024]{2,1,0:T(8,128)(2,1)S(1)} %bitcast.16) | data formatting | bytes 1048576
  43.1 0.8 %copy.18 = bf16[1,256,1024]{2,1,0:T(8,128)(2,1)} copy(bf16[1,256,1024]{2,1,0:T(8,128)(2,1)S(1)} %bitcast.15) | data formatting | bytes 1048576
  43.9 0.8 %copy.19 = f32[512,256]{1,0:T(8,128)} copy(f32[512,256]{1,0:T(8,128)S(1)} %get-tuple-element.14) | data formatting | bytes 1048576
Async XLA Ops:
  0.6 0.7 %copy-start.8 = (f32[1,256,8]{1,2,0:T(8,128)S(1)}, f32[1,256,8]{1,2,0:T(8,128)}, u32[]{:S(2)}) copy-start(f32[1,256,8]{1,2,0:T(8,128)} %param.14) | copy-start | bytes 24580
  1.5 0.7 %copy-start.7 = (s32[1,2]{1,0:T(1,128)S(1)}, s32[1,2]{1,0:T(1,128)}, u32[]{:S(2)}) copy-start(s32[1,2]{1,0:T(1,128)} %off_ref.1) | copy-start | bytes 28
  2.1 1.0 %copy-start = (bf16[2048,128]{1,0:T(8,128)(2,1)S(1)}, bf16[2048,128]{1,0:T(8,128)(2,1)}, u32[]{:S(2)}) copy-start(bf16[2048,128]{1,0:T(8,128)(2,1)} %pi_h.1) | copy-start | bytes 1572868
  3.2 1.0 %copy-start.1 = (bf16[2048,128]{1,0:T(8,128)(2,1)S(1)}, bf16[2048,128]{1,0:T(8,128)(2,1)}, u32[]{:S(2)}) copy-start(bf16[2048,128]{1,0:T(8,128)(2,1)} %po_h.1) | copy-start | bytes 1572868
  4.2 1.0 %copy-start.2 = (bf16[1,256,1024]{2,1,0:T(8,128)(2,1)S(1)}, bf16[1,256,1024]{2,1,0:T(8,128)(2,1)}, u32[]{:S(2)}) copy-start(bf16[1,256,1024]{2,1,0:T(8,128)(2,1)} %param.13) | copy-start | bytes 1572868
  5.2 1.0 %copy-start.3 = (bf16[1,256,1024]{2,1,0:T(8,128)(2,1)S(1)}, bf16[1,256,1024]{2,1,0:T(8,128)(2,1)}, u32[]{:S(2)}) copy-start(bf16[1,256,1024]{2,1,0:T(8,128)(2,1)} %param.15) | copy-start | bytes 1572868
  6.3 1.0 %copy-start.4 = (bf16[1,256,1024]{2,1,0:T(8,128)(2,1)S(1)}, bf16[1,256,1024]{2,1,0:T(8,128)(2,1)}, u32[]{:S(2)}) copy-start(bf16[1,256,1024]{2,1,0:T(8,128)(2,1)} %param.16) | copy-start | bytes 1572868
  7.3 1.0 %copy-start.5 = (bf16[1,256,1024]{2,1,0:T(8,128)(2,1)S(1)}, bf16[1,256,1024]{2,1,0:T(8,128)(2,1)}, u32[]{:S(2)}) copy-start(bf16[1,256,1024]{2,1,0:T(8,128)(2,1)} %param.17) | copy-start | bytes 1572868
  8.4 1.0 %copy-start.6 = (bf16[1,256,1024]{2,1,0:T(8,128)(2,1)S(1)}, bf16[1,256,1024]{2,1,0:T(8,128)(2,1)}, u32[]{:S(2)}) copy-start(bf16[1,256,1024]{2,1,0:T(8,128)(2,1)} %param.18) | copy-start | bytes 1572868

commit v2 on v1

--- a/solution.py
+++ b/solution.py
@@ -13,20 +13,23 @@
 MESH = pl.DeviceIdType.MESH
 BF = jnp.bfloat16
 F32 = jnp.float32
-HI = lax.Precision.HIGHEST
-
-
-def mm(a, b, ca=1, cb=0, precision=None):
-    return lax.dot_general(
-        a, b, (((ca,), (cb,)), ((), ())), preferred_element_type=F32, precision=precision
-    )
+
+
+def mm(a, b, ca=1, cb=0):
+    return lax.dot_general(a, b, (((ca,), (cb,)), ((), ())), preferred_element_type=F32)
+
+
+def three(a):
+    first = a.astype(BF).astype(F32)
+    second = (a - first).astype(BF).astype(F32)
+    return jnp.concatenate([first, second, a - first - second], axis=0).astype(BF)
 
 
 def kernel(
     sizes,
     lat_h, pi_h, po_h, x_h, ld_ref, q_h, k_h, v_h, g_h, off_ref,
     lo_h, ig_h, pg_h,
-    lat, pi, po, x, g, q, kx, vx, lo, ig, pg,
+    lat, pi, po, x, g, q, kx, vx, lo, ig, lat_t,
     cumb, cumt, b_s, c_s, cs_s, kern, wsum, xw, rg, inner, gx, att,
     f_fresh, f_in, f_out, r_fresh, r_in, r_out,
     both, rz, zfull, term, rs, agf,
@@ -35,7 +38,7 @@
 ):
     n_tm, n_z, n_dp = sizes
     rows, width = x.shape
-    heads = ld_ref.shape[1]
+    heads = ld_ref.shape[0]
     dim = width // heads
     states = pi.shape[1]
     scale = 1.0 / math.sqrt(states)
@@ -77,15 +80,15 @@
 
     row_i = lax.broadcasted_iota(jnp.int32, (rows, rows), 0)
     col_i = lax.broadcasted_iota(jnp.int32, (rows, rows), 1)
-    lower = (row_i >= col_i).astype(F32)
-    ld = ld_ref[...]
-    cum = mm(lower, ld, precision=HI)
-    cumt[...] = mm(ld, lower, 0, 1, precision=HI)
+    upper = (row_i <= col_i).astype(BF)
+    sums = mm(three(ld_ref[...]), upper)
+    cum = sums[:heads] + sums[heads : 2 * heads] + sums[2 * heads :]
+    cumt[...] = cum
     spread = (
-        lax.broadcasted_iota(jnp.int32, (heads, width), 1) // dim
-        == lax.broadcasted_iota(jnp.int32, (heads, width), 0)
-    ).astype(F32)
-    cumb[...] = mm(cum, spread, precision=HI)
+        lax.broadcasted_iota(jnp.int32, (3 * heads, width), 1) // dim
+        == lax.rem(lax.broadcasted_iota(jnp.int32, (3 * heads, width), 0), heads)
+    ).astype(BF)
+    cumb[...] = mm(three(cum), spread, 0, 0)
 
     for load in loads[:3]:
         load.wait()
@@ -159,11 +162,6 @@
         @pl.when(rslot == i)
         def _():
             chain_step(rev, rplace, r_fresh, r_out, r_in)
-
-        @pl.when((tm < n_tm - 1) & (i == min(1, steps - 1)))
-        def _():
-            for halo in halos:
-                halo.start()
 
         acc = wsum[...]
         for j in range(per):
@@ -191,26 +189,41 @@
         chain_step(rev, rplace, r_fresh, r_out, r_in)
 
     weigh = (wsum[...] * scale).astype(BF)
-    both[:, :states] = (mm(weigh, c_s[...], 0, 0) + mm(xw[...], r_in[...], 1, 1)).astype(BF)
-    both[:, states:] = (
-        mm(weigh, b_s[...]) + mm(rg[...], f_in[...], 1, 1) * scale
-    ).astype(BF)
-    zscatter = []
-    for k in range(1, n_z):
-        other, to = zmember(k)
-        zscatter.append(
-            pltpu.make_async_remote_copy(
-                src_ref=both.at[pl.ds(pl.multiple_of(other * zrows, zrows), zrows)],
-                dst_ref=rz.at[k - 1], send_sem=zs_send.at[k - 1], recv_sem=zs_recv.at[k - 1],
-                device_id=to, device_id_type=MESH,
+    halves = (1, 0)
+    half_at = [pl.ds(0, states), pl.ds(states, states)]
+    zscatter, zgather, scatter, gather = {}, {}, {}, {}
+    mine = pl.ds(pl.multiple_of(z * zrows, zrows), zrows)
+    for half in halves:
+        if half:
+            rows_grad = mm(weigh, b_s[...]) + mm(rg[...], f_in[...], 1, 1) * scale
+        else:
+            rows_grad = mm(weigh, c_s[...], 0, 0) + mm(xw[...], r_in[...], 1, 1)
+        both[:, half_at[half]] = rows_grad.astype(BF)
+        zscatter[half] = []
+        for k in range(1, n_z):
+            other, to = zmember(k)
+            zscatter[half].append(
+                pltpu.make_async_remote_copy(
+                    src_ref=both.at[
+                        pl.ds(pl.multiple_of(other * zrows, zrows), zrows), half_at[half]
+                    ],
+                    dst_ref=rz.at[half, k - 1],
+                    send_sem=zs_send.at[half, k - 1],
+                    recv_sem=zs_recv.at[half, k - 1],
+                    device_id=to, device_id_type=MESH,
+                )
             )
-        )
-        zscatter[-1].start()
+            zscatter[half][-1].start()
+
+    @pl.when(tm < n_tm - 1)
+    def _():
+        for halo in halos:
+            halo.start()
 
     a_row = lax.broadcasted_iota(jnp.int32, (QB, W + QB), 0)
     a_col = lax.broadcasted_iota(jnp.int32, (QB, W + QB), 1)
 
-    def attend(blk):
+    def attend(blk, put):
         seen = (a_col <= a_row + W) & (a_col >= a_row + 1 + off_ref[0, blk])
         seen = seen & (a_col >= W - (tm * rows + blk * QB))
 
@@ -223,69 +236,39 @@
                 e = jnp.exp((s - top) * (1.0 / math.sqrt(dim)))
                 whole = jnp.sum(e, axis=1, keepdims=True)
                 o = mm(e.astype(BF), vx[blk * QB : blk * QB + W + QB, at])
-                att[blk * QB : (blk + 1) * QB, at] = o / whole
+                put(at, o / whole)
             return 0
 
         lax.fori_loop(0, steps, step, 0)
 
     for blk in range(1, rows // QB):
-        attend(blk)
-
-    mine = pl.ds(pl.multiple_of(z * zrows, zrows), zrows)
-    for copy in zscatter:
-        copy.wait_recv()
-    part = both[mine, :].astype(F32)
-    for k in range(n_z - 1):
-        part = part + rz[k].astype(F32)
-    zfull[mine, :] = part.astype(BF)
-    zgather = []
-    for k in range(1, n_z):
-        other, to = zmember(k)
-        zgather.append(
-            pltpu.make_async_remote_copy(
-                src_ref=zfull.at[mine], dst_ref=zfull.at[mine],
-                send_sem=zg_send.at[k - 1], recv_sem=zg_recv.at[k - 1],
-                device_id=to, device_id_type=MESH,
+        def keep(at, o, blk=blk):
+            att[blk * QB : (blk + 1) * QB, at] = o
+
+        attend(blk, keep)
+    cols = pl.ds(pl.multiple_of(z * share, share), share)
+    lat_t[...] = lat[:, cols].T
+
+    for half in halves:
+        for copy in zscatter[half]:
+            copy.wait_recv()
+        part = both[mine, half_at[half]].astype(F32)
+        for k in range(n_z - 1):
+            part = part + rz[half, k].astype(F32)
+        zfull[mine, half_at[half]] = part.astype(BF)
+        zgather[half] = []
+        for k in range(1, n_z):
+            other, to = zmember(k)
+            zgather[half].append(
+                pltpu.make_async_remote_copy(
+                    src_ref=zfull.at[mine, half_at[half]],
+                    dst_ref=zfull.at[mine, half_at[half]],
+                    send_sem=zg_send.at[half, k - 1],
+                    recv_sem=zg_recv.at[half, k - 1],
+                    device_id=to, device_id_type=MESH,
+                )
             )
-        )
-        zgather[-1].start()
-
-    @pl.when(tm > 0)
-    def _():
-        for halo in halos:
-            halo.wait_recv()
-
-    @pl.when(tm == 0)
-    def _():
-        for buf in (kx, vx):
-            buf[0:W, :] = jnp.zeros((W, width), BF)
-
-    attend(0)
-
-    for copy in zgather:
-        copy.wait_recv()
-    cols = pl.ds(pl.multiple_of(z * share, share), share)
-    grad = mm(lat[:, cols], zfull[...], 0, 0) * (1.0 / math.sqrt(n_dp * rows * n_tm))
-    term[...] = grad.astype(BF)
-    scatter = []
-    for k in range(1, group):
-        other, to = member(k)
-        at = jnp.where(other < owners, other, 0) if owners < group else other
-        copy = pltpu.make_async_remote_copy(
-            src_ref=term.at[pl.ds(pl.multiple_of(at * chunk, chunk), chunk)],
-            dst_ref=rs.at[k - 1], send_sem=rs_send.at[k - 1], recv_sem=rs_recv.at[k - 1],
-            device_id=to, device_id_type=MESH,
-        )
-        scatter.append((other < owners, copy))
-
-    def when(cond, action):
-        if owners == group:
-            action()
-        else:
-            pl.when(cond)(action)
-
-    for cond, copy in scatter:
-        when(cond, copy.start)
+            zgather[half][-1].start()
 
     def finish(i, _):
         for j in range(per):
@@ -293,7 +276,9 @@
             cb = cumb[:, at]
             out = inner[:, at] + jnp.exp(cb) * mm(cs_s[...], f_in[:, at])
             mean = jnp.mean(out * out, axis=1, keepdims=True)
-            lo[:, at] = (out * lax.rsqrt(mean + 1e-05) + att[:, at]).astype(BF)
+            normed = out * lax.rsqrt(mean + 1e-05)
+            inner[0:QB, at] = normed[0:QB]
+            lo[QB:rows, at] = (normed[QB:rows] + att[QB:rows, at]).astype(BF)
             fall = jnp.exp(cb[rows - 1 : rows, :] - cb)
             ig[:, at] = (gx[:, at] + fall * mm(b_s[...], r_in[:, at])).astype(BF)
         return 0
@@ -301,49 +286,77 @@
     lax.fori_loop(0, steps, finish, 0)
     stores = [
         pltpu.make_async_copy(src, dst, store_sem.at[i])
-        for i, (src, dst) in enumerate([(lo, lo_h), (ig, ig_h), (pg, pg_h)])
+        for i, (src, dst) in enumerate([(lo, lo_h), (ig, ig_h), (agf, pg_h)])
     ]
+    stores[1].start()
+
+    def when(cond, action):
+        if owners == group:
+            action()
+        else:
+            pl.when(cond)(action)
+
+    for half in halves:
+        for copy in zgather[half]:
+            copy.wait_recv()
+        grad = mm(lat_t[...], zfull[:, half_at[half]])
+        term[:, half_at[half]] = (grad * (1.0 / math.sqrt(n_dp * rows * n_tm))).astype(BF)
+        scatter[half] = []
+        for k in range(1, group):
+            other, to = member(k)
+            at = jnp.where(other < owners, other, 0) if owners < group else other
+            copy = pltpu.make_async_remote_copy(
+                src_ref=term.at[pl.ds(pl.multiple_of(at * chunk, chunk), chunk), half_at[half]],
+                dst_ref=rs.at[half, k - 1],
+                send_sem=rs_send.at[half, k - 1],
+                recv_sem=rs_recv.at[half, k - 1],
+                device_id=to, device_id_type=MESH,
+            )
+            scatter[half].append((other < owners, copy))
+            when(other < owners, copy.start)
+
+    @pl.when(tm > 0)
+    def _():
+        for halo in halos:
+            halo.wait_recv()
+
+    @pl.when(tm == 0)
+    def _():
+        for buf in (kx, vx):
+            buf[0:W, :] = jnp.zeros((W, width), BF)
+
+    def add(at, o):
+        lo[0:QB, at] = (inner[0:QB, at] + o).astype(BF)
+
+    attend(0, add)
     stores[0].start()
-    stores[1].start()
 
     own = jnp.where(me < owners, me, 0) if owners < group else me
     owned = pl.ds(pl.multiple_of(own * chunk, chunk), chunk)
-    gather = []
-    for k in range(1, group):
-        other, to = member(k)
-        copy = pltpu.make_async_remote_copy(
-            src_ref=agf.at[owned], dst_ref=agf.at[owned],
-            send_sem=ag_send.at[k - 1], recv_sem=ag_recv.at[k - 1],
-            device_id=to, device_id_type=MESH,
-        )
-        gather.append((lax.rem(me + group - k, group) < owners, copy))
-
-    def own_sum():
-        for _, copy in scatter:
+
+    def own_sum(half):
+        for _, copy in scatter[half]:
             copy.wait_recv()
-        part = term[owned, :].astype(F32)
+        part = term[owned, half_at[half]].astype(F32)
         for k in range(group - 1):
-            part = part + rs[k].astype(F32)
-        agf[owned, :] = part.astype(BF)
-        for _, copy in gather:
+            part = part + rs[half, k].astype(F32)
+        agf[owned, half_at[half]] = part.astype(BF)
+        for _, copy in gather[half]:
             copy.start()
 
-    when(me < owners, own_sum)
-    for cond, copy in gather:
-        when(cond, copy.wait_recv)
-    pg[...] = agf[...].astype(F32)
-    stores[2].start()
-
-    for copy in zscatter + zgather:
-        copy.wait_send()
-    for cond, copy in scatter:
-        when(cond, copy.wait_send)
-
-    def gathered():
-        for _, copy in gather:
-            copy.wait_send()
-
-    when(me < owners, gathered)
+    for half in halves:
+        gather[half] = []
+        for k in range(1, group):
+            other, to = member(k)
+            copy = pltpu.make_async_remote_copy(
+                src_ref=agf.at[owned, half_at[half]],
+                dst_ref=agf.at[owned, half_at[half]],
+                send_sem=ag_send.at[half, k - 1],
+                recv_sem=ag_recv.at[half, k - 1],
+                device_id=to, device_id_type=MESH,
+            )
+            gather[half].append((lax.rem(me + group - k, group) < owners, copy))
+        when(me < owners, functools.partial(own_sum, half))
 
     @pl.when(tm < n_tm - 1)
     def _():
@@ -355,6 +368,20 @@
     def _():
         rev.wait_send()
 
+    def gathered(half):
+        for _, copy in gather[half]:
+            copy.wait_send()
+
+    for half in halves:
+        for copy in zscatter[half] + zgather[half]:
+            copy.wait_send()
+        for cond, copy in scatter[half]:
+            when(cond, copy.wait_send)
+    for half in halves:
+        for cond, copy in gather[half]:
+            when(cond, copy.wait_recv)
+        when(me < owners, functools.partial(gathered, half))
+    stores[2].start()
     for store in stores:
         store.wait()
 
@@ -383,7 +410,8 @@
     owners = min(group, share // 16)
     chunk = share // owners
     zrows = rows // n_z
-    hbm = pl.BlockSpec(memory_space=pl.ANY)
+    hbm = pl.BlockSpec(memory_space=pltpu.HBM)
+    anywhere = pl.BlockSpec(memory_space=pl.ANY)
     vmem = pl.BlockSpec(memory_space=pltpu.VMEM)
     smem = pl.BlockSpec(memory_space=pltpu.SMEM)
 
@@ -396,15 +424,15 @@
         out_shape=(
             jax.ShapeDtypeStruct((rows, width), BF),
             jax.ShapeDtypeStruct((rows, width), BF),
-            jax.ShapeDtypeStruct((share, 2 * states), F32),
+            jax.ShapeDtypeStruct((share, 2 * states), BF),
         ),
         in_specs=[hbm, hbm, hbm, hbm, vmem, hbm, hbm, hbm, hbm, smem],
-        out_specs=(hbm, hbm, hbm),
+        out_specs=(anywhere, anywhere, anywhere),
         scratch_shapes=[
             v((rows, model)), v((model, states)), v((model, states)),
             v((rows, width)), v((rows, width)), v((rows, width)),
             v((W + rows, width)), v((W + rows, width)),
-            v((rows, width)), v((rows, width)), v((share, 2 * states), F32),
+            v((rows, width)), v((rows, width)), v((share, rows)),
             v((rows, width), F32), v((heads, rows), F32),
             v((rows, states)), v((rows, states)), v((rows, states)),
             v((rows, rows), F32), v((rows, rows), F32),
@@ -412,20 +440,20 @@
             v((rows, width), F32), v((rows, width), F32), v((rows, width), F32),
             v((states, width), F32), v((states, width)), v((states, width)),
             v((states, width), F32), v((states, width)), v((states, width)),
-            v((rows, 2 * states)), v((n_z - 1, zrows, 2 * states)), v((rows, 2 * states)),
-            v((share, 2 * states)), v((group - 1, chunk, 2 * states)), v((share, 2 * states)),
+            v((rows, 2 * states)), v((2, n_z - 1, zrows, states)), v((rows, 2 * states)),
+            v((share, 2 * states)), v((2, group - 1, chunk, states)), v((share, 2 * states)),
             dma((8,)), dma((3,)), dma((2,)), dma((2,)), dma((2,)), dma((2,)),
-            dma((n_z - 1,)), dma((n_z - 1,)), dma((n_z - 1,)), dma((n_z - 1,)),
-            dma((group - 1,)), dma((group - 1,)), dma((group - 1,)), dma((group - 1,)),
+            dma((2, n_z - 1)), dma((2, n_z - 1)), dma((2, n_z - 1)), dma((2, n_z - 1)),
+            dma((2, group - 1)), dma((2, group - 1)), dma((2, group - 1)), dma((2, group - 1)),
         ],
         compiler_params=pltpu.CompilerParams(
-            collective_id=0, has_side_effects=True, vmem_limit_bytes=48 * 1024 * 1024
+            collective_id=0, has_side_effects=True, vmem_limit_bytes=60 * 1024 * 1024
         ),
     )(
-        latents[0], proj_input, proj_output, scan_input[0], log_decay[0],
+        latents[0], proj_input, proj_output, scan_input[0], log_decay[0].T,
         att_queries[0], att_keys[0], att_values[0], scan_cotangent[0], window_offsets,
     )
-    return layer_out[None], input_grad[None], proj_grad
+    return layer_out[None], input_grad[None], proj_grad.astype(F32)
 
 
 def solution(mesh):

time: 45.2 us -> 37.3 us (0.83)
  local copies, waits for them, and re-layouts: 11.1 us -> 2.03 us
  other arithmetic: 0 us -> 1.84 us
    unnamed x22 -> x6, local copies, waits for them, and re-layouts: 11.1 us -> 2.03 us
    convert_element_type x0 -> x1, other arithmetic: none -> 1.84 us  [on_device(): return (layer_out[None], input_grad[None], proj_grad.astype(F32))]
where the time goes in v2:
time: 37.3 us; the launch traced here: 37.1 us
  Pallas kernels  32.6 us (87%)
  local copies, waits for them, and re-layouts  2.03 us (5%)
  other arithmetic  1.84 us (5%)
  between operations  0.65 us (2%)
    pallas_call x1, Pallas kernels, on_device(): pl.pallas_call(functools.partial(kernel, sizes), out_shape=(jax.ShapeDtyp...  32.6 us
    unnamed x6, local copies, waits for them, and re-layouts  2.03 us
    convert_element_type x1, other arithmetic, on_device(): return (layer_out[None], input_grad[None], proj_grad.astype(F32))  1.84 us

profile of v2, /device:TPU:0, one launch (start us, length us, event | category | flops | bytes accessed | tf_op | source)
XLA Modules:
  0.0 37.1 jit_solution(13209028722820744477)
XLA Ops:
  0.6 32.6 %shard_map.121 = (bf16[256,1024]{1,0:T(8,128)(2,1)}, bf16[256,1024]{1,0:T(8,128)(2,1)}, bf16[512,256]{1,0:T(8,128)(2,1)}) custom-call(bf16[256,2048]{1,0:T(8,128)(2,1)} %bitcast.11, bf16[2048,128]{1,0:T(8,128)(2,1)} %pi_h.1, bf16[2048,128]{1,0:T(8,128)(2,1)} %po_h.1, bf16[256,1024]{1,0:T(8,128)(2,1)} %bitcast.12, f32[8,256]{1,0:T(8,128)} %bitcast.19, ...), custom_call_target="tpu_custom_call" | custom-call | tf_op jit(solution)/shard_map/pallas_call | solution.py:422
  33.2 0.0 copy-start.1
  33.2 1.8 %convert_element_type.3 = f32[512,256]{1,0:T(8,128)} convert(bf16[512,256]{1,0:T(8,128)(2,1)} %get-tuple-element.8) | non-fusion elementwise | flops 131072 | bytes 786432 | tf_op jit(solution)/shard_map/convert_element_type | solution.py:456
  35.1 0.0 copy-done.1
  35.1 0.0 copy-start
  35.1 0.8 %copy.15 = bf16[1,256,1024]{2,1,0:T(8,128)(2,1)} copy(bf16[1,256,1024]{2,1,0:T(8,128)(2,1)S(1)} %bitcast.18) | data formatting | bytes 1048576
  35.9 0.4 %copy-done = bf16[256,1024]{1,0:T(8,128)(2,1)S(1)} copy-done((bf16[256,1024]{1,0:T(8,128)(2,1)S(1)}, bf16[256,1024]{1,0:T(8,128)(2,1)}, u32[]{:S(2)}) %copy-start) | copy-done | bytes 524312
  36.3 0.8 %copy.16 = bf16[1,256,1024]{2,1,0:T(8,128)(2,1)} copy(bf16[1,256,1024]{2,1,0:T(8,128)(2,1)S(1)} %bitcast.17) | data formatting | bytes 1048576
Async XLA Ops:
  33.2 1.8 %copy-start.1 = (bf16[256,1024]{1,0:T(8,128)(2,1)S(1)}, bf16[256,1024]{1,0:T(8,128)(2,1)}, u32[]{:S(2)}) copy-start(bf16[256,1024]{1,0:T(8,128)(2,1)} %get-tuple-element.6) | copy-start | bytes 1572868
  35.1 1.2 %copy-start = (bf16[256,1024]{1,0:T(8,128)(2,1)S(1)}, bf16[256,1024]{1,0:T(8,128)(2,1)}, u32[]{:S(2)}) copy-start(bf16[256,1024]{1,0:T(8,128)(2,1)} %get-tuple-element.7) | copy-start | bytes 1572868

commit v3 on v2

--- a/solution.py
+++ b/solution.py
@@ -134,8 +134,26 @@
             copy.start()
 
     rplace = n_tm - 1 - tm
-    fslot = jnp.where(tm < 2, tm, 2 * tm - 1)
-    rslot = jnp.where(rplace < 2, rplace, 2 * rplace - 1)
+    early_fwd = 2 * tm < n_tm
+    half_of = [jnp.where(early_fwd, 1, 0), jnp.where(early_fwd, 0, 1)]
+
+    def early_step(ready):
+        @pl.when(early_fwd & ready(tm))
+        def _():
+            chain_step(fwd, tm, f_fresh, f_out, f_in)
+
+        @pl.when(jnp.logical_not(early_fwd) & ready(rplace))
+        def _():
+            chain_step(rev, rplace, r_fresh, r_out, r_in)
+
+    def late_step(ready):
+        @pl.when(early_fwd & ready(rplace))
+        def _():
+            chain_step(rev, rplace, r_fresh, r_out, r_in)
+
+        @pl.when(jnp.logical_not(early_fwd) & ready(tm))
+        def _():
+            chain_step(fwd, tm, f_fresh, f_out, f_in)
 
     halos = [
         pltpu.make_async_remote_copy(
@@ -155,13 +173,7 @@
         return pl.ds(pl.multiple_of(h * dim, dim), dim)
 
     def local_step(i, _):
-        @pl.when(fslot == i)
-        def _():
-            chain_step(fwd, tm, f_fresh, f_out, f_in)
-
-        @pl.when(rslot == i)
-        def _():
-            chain_step(rev, rplace, r_fresh, r_out, r_in)
+        early_step(lambda place: place == i)
 
         acc = wsum[...]
         for j in range(per):
@@ -180,50 +192,85 @@
 
     lax.fori_loop(0, steps, local_step, 0)
 
-    @pl.when(fslot >= steps)
-    def _():
-        chain_step(fwd, tm, f_fresh, f_out, f_in)
-
-    @pl.when(rslot >= steps)
-    def _():
-        chain_step(rev, rplace, r_fresh, r_out, r_in)
+    early_step(lambda place: place >= steps)
 
     weigh = (wsum[...] * scale).astype(BF)
-    halves = (1, 0)
-    half_at = [pl.ds(0, states), pl.ds(states, states)]
-    zscatter, zgather, scatter, gather = {}, {}, {}, {}
+    zscatter, zgather, scatter, gather = [[], []], [[], []], [[], []], [[], []]
     mine = pl.ds(pl.multiple_of(z * zrows, zrows), zrows)
-    for half in halves:
-        if half:
-            rows_grad = mm(weigh, b_s[...]) + mm(rg[...], f_in[...], 1, 1) * scale
-        else:
-            rows_grad = mm(weigh, c_s[...], 0, 0) + mm(xw[...], r_in[...], 1, 1)
-        both[:, half_at[half]] = rows_grad.astype(BF)
-        zscatter[half] = []
+    cols = pl.ds(pl.multiple_of(z * share, share), share)
+
+    def fill_c():
+        both[1] = (mm(weigh, b_s[...]) + mm(rg[...], f_in[...], 1, 1) * scale).astype(BF)
+
+    def fill_b():
+        both[0] = (mm(weigh, c_s[...], 0, 0) + mm(xw[...], r_in[...], 1, 1)).astype(BF)
+
+    def start_zscatter(turn):
+        c_now = early_fwd if turn == 0 else jnp.logical_not(early_fwd)
+        pl.when(c_now)(fill_c)
+        pl.when(jnp.logical_not(c_now))(fill_b)
+        half = half_of[turn]
         for k in range(1, n_z):
             other, to = zmember(k)
-            zscatter[half].append(
-                pltpu.make_async_remote_copy(
-                    src_ref=both.at[
-                        pl.ds(pl.multiple_of(other * zrows, zrows), zrows), half_at[half]
-                    ],
-                    dst_ref=rz.at[half, k - 1],
-                    send_sem=zs_send.at[half, k - 1],
-                    recv_sem=zs_recv.at[half, k - 1],
-                    device_id=to, device_id_type=MESH,
-                )
+            copy = pltpu.make_async_remote_copy(
+                src_ref=both.at[half, pl.ds(pl.multiple_of(other * zrows, zrows), zrows)],
+                dst_ref=rz.at[half, k - 1],
+                send_sem=zs_send.at[half, k - 1],
+                recv_sem=zs_recv.at[half, k - 1],
+                device_id=to, device_id_type=MESH,
             )
-            zscatter[half][-1].start()
-
-    @pl.when(tm < n_tm - 1)
-    def _():
-        for halo in halos:
-            halo.start()
+            zscatter[turn].append(copy)
+            copy.start()
+
+    def start_zgather(turn):
+        half = half_of[turn]
+        for copy in zscatter[turn]:
+            copy.wait_recv()
+        part = both[half, mine, :].astype(F32)
+        for k in range(n_z - 1):
+            part = part + rz[half, k].astype(F32)
+        zfull[half, mine, :] = part.astype(BF)
+        for k in range(1, n_z):
+            other, to = zmember(k)
+            copy = pltpu.make_async_remote_copy(
+                src_ref=zfull.at[half, mine],
+                dst_ref=zfull.at[half, mine],
+                send_sem=zg_send.at[half, k - 1],
+                recv_sem=zg_recv.at[half, k - 1],
+                device_id=to, device_id_type=MESH,
+            )
+            zgather[turn].append(copy)
+            copy.start()
+
+    def when(cond, action):
+        if owners == group:
+            action()
+        else:
+            pl.when(cond)(action)
+
+    def start_scatter(turn):
+        half = half_of[turn]
+        for copy in zgather[turn]:
+            copy.wait_recv()
+        grad = mm(lat_t[...], zfull[half])
+        term[half] = (grad * (1.0 / math.sqrt(n_dp * rows * n_tm))).astype(BF)
+        for k in range(1, group):
+            other, to = member(k)
+            at = jnp.where(other < owners, other, 0) if owners < group else other
+            copy = pltpu.make_async_remote_copy(
+                src_ref=term.at[half, pl.ds(pl.multiple_of(at * chunk, chunk), chunk)],
+                dst_ref=rs.at[half, k - 1],
+                send_sem=rs_send.at[half, k - 1],
+                recv_sem=rs_recv.at[half, k - 1],
+                device_id=to, device_id_type=MESH,
+            )
+            scatter[turn].append((other < owners, copy))
+            when(other < owners, copy.start)
 
     a_row = lax.broadcasted_iota(jnp.int32, (QB, W + QB), 0)
     a_col = lax.broadcasted_iota(jnp.int32, (QB, W + QB), 1)
 
-    def attend(blk, put):
+    def attend(blk, put, low, high):
         seen = (a_col <= a_row + W) & (a_col >= a_row + 1 + off_ref[0, blk])
         seen = seen & (a_col >= W - (tm * rows + blk * QB))
 
@@ -239,36 +286,14 @@
                 put(at, o / whole)
             return 0
 
-        lax.fori_loop(0, steps, step, 0)
-
-    for blk in range(1, rows // QB):
-        def keep(at, o, blk=blk):
-            att[blk * QB : (blk + 1) * QB, at] = o
-
-        attend(blk, keep)
-    cols = pl.ds(pl.multiple_of(z * share, share), share)
-    lat_t[...] = lat[:, cols].T
-
-    for half in halves:
-        for copy in zscatter[half]:
-            copy.wait_recv()
-        part = both[mine, half_at[half]].astype(F32)
-        for k in range(n_z - 1):
-            part = part + rz[half, k].astype(F32)
-        zfull[mine, half_at[half]] = part.astype(BF)
-        zgather[half] = []
-        for k in range(1, n_z):
-            other, to = zmember(k)
-            zgather[half].append(
-                pltpu.make_async_remote_copy(
-                    src_ref=zfull.at[mine, half_at[half]],
-                    dst_ref=zfull.at[mine, half_at[half]],
-                    send_sem=zg_send.at[half, k - 1],
-                    recv_sem=zg_recv.at[half, k - 1],
-                    device_id=to, device_id_type=MESH,
-                )
-            )
-            zgather[half][-1].start()
+        lax.fori_loop(low, high, step, 0)
+
+    def attend_own(low, high):
+        for blk in range(1, rows // QB):
+            def keep(at, o, blk=blk):
+                att[blk * QB : (blk + 1) * QB, at] = o
+
+            attend(blk, keep, low, high)
 
     def finish(i, _):
         for j in range(per):
@@ -283,37 +308,33 @@
             ig[:, at] = (gx[:, at] + fall * mm(b_s[...], r_in[:, at])).astype(BF)
         return 0
 
-    lax.fori_loop(0, steps, finish, 0)
+    def add(at, o):
+        lo[0:QB, at] = (inner[0:QB, at] + o).astype(BF)
+
     stores = [
         pltpu.make_async_copy(src, dst, store_sem.at[i])
         for i, (src, dst) in enumerate([(lo, lo_h), (ig, ig_h), (agf, pg_h)])
     ]
+
+    start_zscatter(0)
+
+    @pl.when(tm < n_tm - 1)
+    def _():
+        for halo in halos:
+            halo.start()
+
+    attend_own(0, steps // 2)
+    late_step(lambda place: place <= 2)
+    attend_own(steps // 2, steps)
+    lat_t[...] = lat[:, cols].T
+    start_zgather(0)
+    late_step(lambda place: place > 2)
+    start_zscatter(1)
+    start_scatter(0)
+    lax.fori_loop(0, steps // 2, finish, 0)
+    start_zgather(1)
+    lax.fori_loop(steps // 2, steps, finish, 0)
     stores[1].start()
-
-    def when(cond, action):
-        if owners == group:
-            action()
-        else:
-            pl.when(cond)(action)
-
-    for half in halves:
-        for copy in zgather[half]:
-            copy.wait_recv()
-        grad = mm(lat_t[...], zfull[:, half_at[half]])
-        term[:, half_at[half]] = (grad * (1.0 / math.sqrt(n_dp * rows * n_tm))).astype(BF)
-        scatter[half] = []
-        for k in range(1, group):
-            other, to = member(k)
-            at = jnp.where(other < owners, other, 0) if owners < group else other
-            copy = pltpu.make_async_remote_copy(
-                src_ref=term.at[pl.ds(pl.multiple_of(at * chunk, chunk), chunk), half_at[half]],
-                dst_ref=rs.at[half, k - 1],
-                send_sem=rs_send.at[half, k - 1],
-                recv_sem=rs_recv.at[half, k - 1],
-                device_id=to, device_id_type=MESH,
-            )
-            scatter[half].append((other < owners, copy))
-            when(other < owners, copy.start)
 
     @pl.when(tm > 0)
     def _():
@@ -325,38 +346,36 @@
         for buf in (kx, vx):
             buf[0:W, :] = jnp.zeros((W, width), BF)
 
-    def add(at, o):
-        lo[0:QB, at] = (inner[0:QB, at] + o).astype(BF)
-
-    attend(0, add)
+    start_scatter(1)
+    attend(0, add, 0, steps)
     stores[0].start()
 
     own = jnp.where(me < owners, me, 0) if owners < group else me
     owned = pl.ds(pl.multiple_of(own * chunk, chunk), chunk)
-
-    def own_sum(half):
-        for _, copy in scatter[half]:
-            copy.wait_recv()
-        part = term[owned, half_at[half]].astype(F32)
-        for k in range(group - 1):
-            part = part + rs[half, k].astype(F32)
-        agf[owned, half_at[half]] = part.astype(BF)
-        for _, copy in gather[half]:
-            copy.start()
-
-    for half in halves:
-        gather[half] = []
+    for copies in scatter:
+        for _, copy in copies:
+            when(me < owners, copy.wait_recv)
+    for half in range(2):
         for k in range(1, group):
             other, to = member(k)
             copy = pltpu.make_async_remote_copy(
-                src_ref=agf.at[owned, half_at[half]],
-                dst_ref=agf.at[owned, half_at[half]],
+                src_ref=agf.at[half, owned],
+                dst_ref=agf.at[half, owned],
                 send_sem=ag_send.at[half, k - 1],
                 recv_sem=ag_recv.at[half, k - 1],
                 device_id=to, device_id_type=MESH,
             )
             gather[half].append((lax.rem(me + group - k, group) < owners, copy))
-        when(me < owners, functools.partial(own_sum, half))
+
+        def own_sum(half=half):
+            part = term[half, owned, :].astype(F32)
+            for k in range(group - 1):
+                part = part + rs[half, k].astype(F32)
+            agf[half, owned, :] = part.astype(BF)
+            for _, copy in gather[half]:
+                copy.start()
+
+        when(me < owners, own_sum)
 
     @pl.when(tm < n_tm - 1)
     def _():
@@ -368,22 +387,34 @@
     def _():
         rev.wait_send()
 
-    def gathered(half):
-        for _, copy in gather[half]:
+    for turn in range(2):
+        for copy in zscatter[turn] + zgather[turn]:
             copy.wait_send()
-
-    for half in halves:
-        for copy in zscatter[half] + zgather[half]:
-            copy.wait_send()
-        for cond, copy in scatter[half]:
+        for cond, copy in scatter[turn]:
             when(cond, copy.wait_send)
-    for half in halves:
+    for half in range(2):
         for cond, copy in gather[half]:
             when(cond, copy.wait_recv)
-        when(me < owners, functools.partial(gathered, half))
     stores[2].start()
+    for half in range(2):
+        for _, copy in gather[half]:
+            when(me < owners, copy.wait_send)
     for store in stores:
         store.wait()
+
+
+def hand_out(lo_h, ig_h, pg_ref, lo_out, ig_out, pg_out, sem):
+    copies = [
+        pltpu.make_async_copy(lo_h, lo_out, sem.at[0]),
+        pltpu.make_async_copy(ig_h, ig_out, sem.at[1]),
+    ]
+    for copy in copies:
+        copy.start()
+    for half in range(2):
+        states = pg_ref.shape[2]
+        pg_out[:, half * states : (half + 1) * states] = pg_ref[half].astype(F32)
+    for copy in copies:
+        copy.wait()
 
 
 def on_device(
@@ -424,7 +455,7 @@
         out_shape=(
             jax.ShapeDtypeStruct((rows, width), BF),
             jax.ShapeDtypeStruct((rows, width), BF),
-            jax.ShapeDtypeStruct((share, 2 * states), BF),
+            jax.ShapeDtypeStruct((2, share, states), BF),
         ),
         in_specs=[hbm, hbm, hbm, hbm, vmem, hbm, hbm, hbm, hbm, smem],
         out_specs=(anywhere, anywhere, anywhere),
@@ -440,8 +471,8 @@
             v((rows, width), F32), v((rows, width), F32), v((rows, width), F32),
             v((states, width), F32), v((states, width)), v((states, width)),
             v((states, width), F32), v((states, width)), v((states, width)),
-            v((rows, 2 * states)), v((2, n_z - 1, zrows, states)), v((rows, 2 * states)),
-            v((share, 2 * states)), v((2, group - 1, chunk, states)), v((share, 2 * states)),
+            v((2, rows, states)), v((2, n_z - 1, zrows, states)), v((2, rows, states)),
+            v((2, share, states)), v((2, group - 1, chunk, states)), v((2, share, states)),
             dma((8,)), dma((3,)), dma((2,)), dma((2,)), dma((2,)), dma((2,)),
             dma((2, n_z - 1)), dma((2, n_z - 1)), dma((2, n_z - 1)), dma((2, n_z - 1)),
             dma((2, group - 1)), dma((2, group - 1)), dma((2, group - 1)), dma((2, group - 1)),
@@ -453,7 +484,19 @@
         latents[0], proj_input, proj_output, scan_input[0], log_decay[0].T,
         att_queries[0], att_keys[0], att_values[0], scan_cotangent[0], window_offsets,
     )
-    return layer_out[None], input_grad[None], proj_grad.astype(F32)
+    layer_out, input_grad, proj_grad = pl.pallas_call(
+        hand_out,
+        out_shape=(
+            jax.ShapeDtypeStruct((rows, width), BF),
+            jax.ShapeDtypeStruct((rows, width), BF),
+            jax.ShapeDtypeStruct((share, 2 * states), F32),
+        ),
+        in_specs=[hbm, hbm, vmem],
+        out_specs=(hbm, hbm, vmem),
+        scratch_shapes=[dma((2,))],
+        compiler_params=pltpu.CompilerParams(vmem_limit_bytes=60 * 1024 * 1024),
+    )(layer_out, input_grad, proj_grad)
+    return layer_out[None], input_grad[None], proj_grad
 
 
 def solution(mesh):

time: 37.3 us -> 68.3 us (1.83)
  Pallas kernels: 32.6 us -> 67.5 us
  local copies, waits for them, and re-layouts: 2.03 us -> 0 us
  other arithmetic: 1.84 us -> 0 us
    pallas_call x0 -> x1, Pallas kernels: none -> 34.6 us  [on_device(): pl.pallas_call(hand_out, out_shape=(jax.ShapeDtypeStruct((rows, width), B...]
    unnamed x6 -> x0, local copies, waits for them, and re-layouts: 2.03 us -> none
    convert_element_type x1 -> x0, other arithmetic: 1.84 us -> none  [on_device(): return (layer_out[None], input_grad[None], proj_grad.astype(F32))]
where the time goes in v3:
time: 68.3 us; the launch traced here: 68.1 us
  Pallas kernels  67.5 us (99%)
    pallas_call x1, Pallas kernels, on_device(): pl.pallas_call(hand_out, out_shape=(jax.ShapeDtypeStruct((rows, width), B...  34.6 us
    pallas_call x1, Pallas kernels, on_device(): pl.pallas_call(functools.partial(kernel, sizes), out_shape=(jax.ShapeDtyp...  32.9 us

profile of v3, /device:TPU:0, one launch (start us, length us, event | category | flops | bytes accessed | tf_op | source)
XLA Modules:
  0.0 68.1 jit_solution(1794610851142176795)
XLA Ops:
  0.6 32.9 %shard_map.121 = (bf16[256,1024]{1,0:T(8,128)(2,1)}, bf16[256,1024]{1,0:T(8,128)(2,1)}, bf16[2,512,128]{2,1,0:T(8,128)(2,1)}) custom-call(bf16[256,2048]{1,0:T(8,128)(2,1)} %bitcast.11, bf16[2048,128]{1,0:T(8,128)(2,1)} %pi_h.1, bf16[2048,128]{1,0:T(8,128)(2,1)} %po_h.1, bf16[256,1024]{1,0:T(8,128)(2,1)} %bitcast.12, f32[8,256]{1,0:T(8,128)} %bitcast.17, ...), custom_call_target="tpu_custom_call" | custom-call | tf_op jit(solution)/shard_map/pallas_call | solution.py:453
  33.5 34.6 %shard_map.122 = (bf16[256,1024]{1,0:T(8,128)(2,1)}, bf16[256,1024]{1,0:T(8,128)(2,1)}, f32[512,256]{1,0:T(8,128)}) custom-call(bf16[256,1024]{1,0:T(8,128)(2,1)} %get-tuple-element.9.lo_h, bf16[256,1024]{1,0:T(8,128)(2,1)} %get-tuple-element.10.ig_h, bf16[2,512,128]{2,1,0:T(8,128)(2,1)} %get-tuple-element.11.pg_ref), custom_call_target="tpu_custom_call" | custom-call | tf_op jit(solution)/shard_map/pallas_call | solution.py:487

commit v4 on v3

--- a/solution.py
+++ b/solution.py
@@ -29,7 +29,7 @@
     sizes,
     lat_h, pi_h, po_h, x_h, ld_ref, q_h, k_h, v_h, g_h, off_ref,
     lo_h, ig_h, pg_h,
-    lat, pi, po, x, g, q, kx, vx, lo, ig, lat_t,
+    lat, proj, x, g, q, kx, vx, lo, ig, lat_t,
     cumb, cumt, b_s, c_s, cs_s, kern, wsum, xw, rg, inner, gx, att,
     f_fresh, f_in, f_out, r_fresh, r_in, r_out,
     both, rz, zfull, term, rs, agf,
@@ -40,7 +40,7 @@
     rows, width = x.shape
     heads = ld_ref.shape[0]
     dim = width // heads
-    states = pi.shape[1]
+    states = proj.shape[1] // 2
     scale = 1.0 / math.sqrt(states)
     group = n_tm * n_dp
     share = lat.shape[1] // n_z
@@ -64,7 +64,8 @@
         pltpu.make_async_copy(src, dst, load_sem.at[i])
         for i, (src, dst) in enumerate(
             [
-                (lat_h, lat), (pi_h, pi), (po_h, po), (x_h, x), (g_h, g),
+                (lat_h, lat), (pi_h, proj.at[:, 0:states]),
+                (po_h, proj.at[:, states : 2 * states]), (x_h, x), (g_h, g),
                 (k_h, kx.at[pl.ds(W, rows)]), (v_h, vx.at[pl.ds(W, rows)]), (q_h, q),
             ]
         )
@@ -92,11 +93,10 @@
 
     for load in loads[:3]:
         load.wait()
-    b_s[...] = mm(lat[...], pi[...]).astype(BF)
-    cf = mm(lat[...], po[...]).astype(BF)
-    c_s[...] = cf
-    cs_s[...] = (cf.astype(F32) * scale).astype(BF)
-    kern[...] = mm(cf, b_s[...], 1, 1) * scale
+    bc = mm(lat[...], proj[...]).astype(BF)
+    b_s[...] = bc[:, :states]
+    c_s[...] = bc[:, states:]
+    cs_s[...] = (bc[:, states:].astype(F32) * scale).astype(BF)
 
     for load in loads[3:5]:
         load.wait()
@@ -163,31 +163,50 @@
         )
         for i, buf in enumerate((kx, vx))
     ]
-    per = 2 if heads % 2 == 0 else 1
+    per = 4 if heads % 4 == 0 else heads
     steps = heads // per
+    early_step(lambda place: place == 0)
+    kern[...] = mm(cs_s[...], b_s[...], 1, 1)
     wsum[...] = jnp.zeros_like(wsum)
     for load in loads[5:]:
         load.wait()
 
+    assert rows == 2 * dim
+    tri = lax.broadcasted_iota(jnp.int32, (dim, dim), 0) >= lax.broadcasted_iota(
+        jnp.int32, (dim, dim), 1
+    )
+
     def lanes(h):
         return pl.ds(pl.multiple_of(h * dim, dim), dim)
 
     def local_step(i, _):
-        early_step(lambda place: place == i)
-
-        acc = wsum[...]
+        early_step(lambda place: (place == i) & (i > 0))
+
+        w00, w10, w11 = wsum[:dim, :dim], wsum[dim:, :dim], wsum[dim:, dim:]
         for j in range(per):
             h = i * per + j
             at = lanes(h)
-            cb = cumb[:, at]
-            gap = jnp.concatenate([cb] * (rows // dim), axis=1) - cumt[pl.ds(h, 1), :]
-            decay = jnp.exp(jnp.where(row_i >= col_i, gap, -jnp.inf))
-            mixing = (kern[...] * decay).astype(BF)
+            ct = cumt[pl.ds(h, 1), :]
+            cb0, cb1 = cumb[:dim, at], cumb[dim:, at]
+            d00 = jnp.exp(jnp.where(tri, cb0 - ct[:, :dim], -jnp.inf))
+            d10 = jnp.exp(cb1 - ct[:, :dim])
+            d11 = jnp.exp(jnp.where(tri, cb1 - ct[:, dim:], -jnp.inf))
+            m00 = (kern[:dim, :dim] * d00).astype(BF)
+            m10 = (kern[dim:, :dim] * d10).astype(BF)
+            m11 = (kern[dim:, dim:] * d11).astype(BF)
             xh, gh = x[:, at], g[:, at]
-            acc = acc + mm(gh, xh, 1, 1) * decay
-            inner[:, at] = mm(mixing, xh)
-            gx[:, at] = mm(mixing, gh, 0, 0)
-        wsum[...] = acc
+            p00 = mm(gh[:dim], xh[:dim], 1, 1)
+            p1 = mm(gh[dim:], xh, 1, 1)
+            w00 = w00 + p00 * d00
+            w10 = w10 + p1[:, :dim] * d10
+            w11 = w11 + p1[:, dim:] * d11
+            inner[:dim, at] = mm(m00, xh[:dim])
+            inner[dim:, at] = mm(jnp.concatenate([m10, m11], axis=1), xh)
+            gx[:dim, at] = mm(jnp.concatenate([m00, m10], axis=0), gh, 0, 0)
+            gx[dim:, at] = mm(m11, gh[dim:], 0, 0)
+        wsum[:dim, :dim] = w00
+        wsum[dim:, :dim] = w10
+        wsum[dim:, dim:] = w11
         return 0
 
     lax.fori_loop(0, steps, local_step, 0)
@@ -347,8 +366,7 @@
             buf[0:W, :] = jnp.zeros((W, width), BF)
 
     start_scatter(1)
-    attend(0, add, 0, steps)
-    stores[0].start()
+    attend(0, add, 0, (steps + 1) // 2)
 
     own = jnp.where(me < owners, me, 0) if owners < group else me
     owned = pl.ds(pl.multiple_of(own * chunk, chunk), chunk)
@@ -377,6 +395,9 @@
 
         when(me < owners, own_sum)
 
+    attend(0, add, (steps + 1) // 2, steps)
+    stores[0].start()
+
     @pl.when(tm < n_tm - 1)
     def _():
         fwd.wait_send()
@@ -403,16 +424,17 @@
         store.wait()
 
 
-def hand_out(lo_h, ig_h, pg_ref, lo_out, ig_out, pg_out, sem):
+def hand_out(lo_ref, ig_ref, pg_ref, lo_out, ig_out, pg_out, pg, sem):
     copies = [
-        pltpu.make_async_copy(lo_h, lo_out, sem.at[0]),
-        pltpu.make_async_copy(ig_h, ig_out, sem.at[1]),
+        pltpu.make_async_copy(src, dst, sem.at[i])
+        for i, (src, dst) in enumerate([(lo_ref, lo_out), (ig_ref, ig_out), (pg, pg_out)])
     ]
-    for copy in copies:
-        copy.start()
+    copies[0].start()
+    copies[1].start()
+    states = pg_ref.shape[2]
     for half in range(2):
-        states = pg_ref.shape[2]
-        pg_out[:, half * states : (half + 1) * states] = pg_ref[half].astype(F32)
+        pg[:, half * states : (half + 1) * states] = pg_ref[half].astype(F32)
+    copies[2].start()
     for copy in copies:
         copy.wait()
 
@@ -460,7 +482,7 @@
         in_specs=[hbm, hbm, hbm, hbm, vmem, hbm, hbm, hbm, hbm, smem],
         out_specs=(anywhere, anywhere, anywhere),
         scratch_shapes=[
-            v((rows, model)), v((model, states)), v((model, states)),
+            v((rows, model)), v((model, 2 * states)),
             v((rows, width)), v((rows, width)), v((rows, width)),
             v((W + rows, width)), v((W + rows, width)),
             v((rows, width)), v((rows, width)), v((share, rows)),
@@ -491,9 +513,9 @@
             jax.ShapeDtypeStruct((rows, width), BF),
             jax.ShapeDtypeStruct((share, 2 * states), F32),
         ),
-        in_specs=[hbm, hbm, vmem],
-        out_specs=(hbm, hbm, vmem),
-        scratch_shapes=[dma((2,))],
+        in_specs=[vmem, vmem, vmem],
+        out_specs=(hbm, hbm, hbm),
+        scratch_shapes=[v((share, 2 * states), F32), dma((3,))],
         compiler_params=pltpu.CompilerParams(vmem_limit_bytes=60 * 1024 * 1024),
     )(layer_out, input_grad, proj_grad)
     return layer_out[None], input_grad[None], proj_grad

time: 68.3 us -> 35.5 us (0.52)
  Pallas kernels: 67.5 us -> 34.6 us
    pallas_call x1, Pallas kernels: 34.6 us -> 2.43 us  [on_device(): pl.pallas_call(hand_out, out_shape=(jax.ShapeDtypeStruct((rows, width), B...]
where the time goes in v4:
time: 35.5 us; the launch traced here: 35.2 us
  Pallas kernels  34.6 us (97%)
  between operations  0.64 us (2%)
    pallas_call x1, Pallas kernels, on_device(): pl.pallas_call(functools.partial(kernel, sizes), out_shape=(jax.ShapeDtyp...  32.2 us
    pallas_call x1, Pallas kernels, on_device(): pl.pallas_call(hand_out, out_shape=(jax.ShapeDtypeStruct((rows, width), B...  2.43 us

profile of v4, /device:TPU:0, one launch (start us, length us, event | category | flops | bytes accessed | tf_op | source)
XLA Modules:
  0.0 35.2 jit_solution(4201440794736453618)
XLA Ops:
  0.6 32.2 %shard_map.121 = (bf16[256,1024]{1,0:T(8,128)(2,1)}, bf16[256,1024]{1,0:T(8,128)(2,1)}, bf16[2,512,128]{2,1,0:T(8,128)(2,1)}) custom-call(bf16[256,2048]{1,0:T(8,128)(2,1)} %bitcast.11, bf16[2048,128]{1,0:T(8,128)(2,1)} %pi_h.1, bf16[2048,128]{1,0:T(8,128)(2,1)} %po_h.1, bf16[256,1024]{1,0:T(8,128)(2,1)} %bitcast.12, f32[8,256]{1,0:T(8,128)} %bitcast.17, ...), custom_call_target="tpu_custom_call" | custom-call | tf_op jit(solution)/shard_map/pallas_call | solution.py:475
  32.8 2.4 %shard_map.122 = (bf16[256,1024]{1,0:T(8,128)(2,1)}, bf16[256,1024]{1,0:T(8,128)(2,1)}, f32[512,256]{1,0:T(8,128)}) custom-call(bf16[256,1024]{1,0:T(8,128)(2,1)} %get-tuple-element.9.lo_ref, bf16[256,1024]{1,0:T(8,128)(2,1)} %get-tuple-element.10.ig_ref, bf16[2,512,128]{2,1,0:T(8,128)(2,1)} %get-tuple-element.11.pg_ref), custom_call_target="tpu_custom_call" | custom-call | tf_op jit(solution)/shard_map/pallas_call | solution.py:509

commit v5 on v4

--- a/solution.py
+++ b/solution.py
@@ -28,12 +28,12 @@
 def kernel(
     sizes,
     lat_h, pi_h, po_h, x_h, ld_ref, q_h, k_h, v_h, g_h, off_ref,
-    lo_h, ig_h, pg_h,
-    lat, proj, x, g, q, kx, vx, lo, ig, lat_t,
+    lo, ig, pg_out,
+    lat, proj, x, g, q, kx, vx, lat_t,
     cumb, cumt, b_s, c_s, cs_s, kern, wsum, xw, rg, inner, gx, att,
     f_fresh, f_in, f_out, r_fresh, r_in, r_out,
     both, rz, zfull, term, rs, agf,
-    load_sem, store_sem, chain_send, chain_recv, halo_send, halo_recv,
+    load_sem, chain_send, chain_recv, halo_send, halo_recv,
     zs_send, zs_recv, zg_send, zg_recv, rs_send, rs_recv, ag_send, ag_recv,
 ):
     n_tm, n_z, n_dp = sizes
@@ -70,7 +70,7 @@
             ]
         )
     ]
-    for load in loads:
+    for load in loads[3:5] + loads[:3]:
         load.start()
 
     barrier = pltpu.get_barrier_semaphore()
@@ -91,47 +91,55 @@
     ).astype(BF)
     cumb[...] = mm(three(cum), spread, 0, 0)
 
+    for load in loads[3:5]:
+        load.wait()
+    for load in loads[5:]:
+        load.start()
+    total = cumb[rows - 1 : rows, :]
+    rg[...] = (jnp.exp(cumb[...]) * g[...].astype(F32)).astype(BF)
+    xw[...] = (jnp.exp(total - cumb[...]) * x[...].astype(F32)).astype(BF)
     for load in loads[:3]:
         load.wait()
     bc = mm(lat[...], proj[...]).astype(BF)
     b_s[...] = bc[:, :states]
     c_s[...] = bc[:, states:]
     cs_s[...] = (bc[:, states:].astype(F32) * scale).astype(BF)
-
-    for load in loads[3:5]:
-        load.wait()
-    total = cumb[rows - 1 : rows, :]
-    rg[...] = (jnp.exp(cumb[...]) * g[...].astype(F32)).astype(BF)
-    xw[...] = (jnp.exp(total - cumb[...]) * x[...].astype(F32)).astype(BF)
     f_fresh[...] = mm(b_s[...], xw[...], 0, 0)
     r_fresh[...] = mm(cs_s[...], rg[...], 0, 0)
     pl.semaphore_wait(barrier, group - 1 + n_z - 1)
 
-    def chain(i, fresh, src, dst, to):
-        return pltpu.make_async_remote_copy(
-            src_ref=src, dst_ref=dst, send_sem=chain_send.at[i], recv_sem=chain_recv.at[i],
-            device_id={"tm": to}, device_id_type=MESH,
-        )
-
     up = lax.rem(tm + 1, n_tm)
     down = lax.rem(tm + n_tm - 1, n_tm)
-    fwd = chain(0, f_fresh, f_out, f_in, up)
-    rev = chain(1, r_fresh, r_out, r_in, down)
-
-    def chain_step(copy, place, fresh, src, dst):
+    pieces = [pl.ds(0, width // 2), pl.ds(width // 2, width // 2)]
+
+    def chain(i, src, dst, to):
+        return [
+            pltpu.make_async_remote_copy(
+                src_ref=src.at[:, at], dst_ref=dst.at[:, at],
+                send_sem=chain_send.at[i, p], recv_sem=chain_recv.at[i, p],
+                device_id={"tm": to}, device_id_type=MESH,
+            )
+            for p, at in enumerate(pieces)
+        ]
+
+    fwd = chain(0, f_out, f_in, up)
+    rev = chain(1, r_out, r_in, down)
+
+    def chain_step(copies, place, fresh, src, dst):
         @pl.when(place == 0)
         def _():
             dst[...] = jnp.zeros_like(dst)
 
-        @pl.when(place > 0)
-        def _():
-            copy.wait_recv()
-
-        @pl.when(place < n_tm - 1)
-        def _():
-            carried = jnp.exp(cumb[rows - 1 : rows, :])
-            src[...] = (carried * dst[...].astype(F32) + fresh[...]).astype(BF)
-            copy.start()
+        for copy, at in zip(copies, pieces):
+            @pl.when(place > 0)
+            def _(copy=copy):
+                copy.wait_recv()
+
+            @pl.when(place < n_tm - 1)
+            def _(copy=copy, at=at):
+                carried = jnp.exp(cumb[rows - 1 : rows, at])
+                src[:, at] = (carried * dst[:, at].astype(F32) + fresh[:, at]).astype(BF)
+                copy.start()
 
     rplace = n_tm - 1 - tm
     early_fwd = 2 * tm < n_tm
@@ -330,11 +338,6 @@
     def add(at, o):
         lo[0:QB, at] = (inner[0:QB, at] + o).astype(BF)
 
-    stores = [
-        pltpu.make_async_copy(src, dst, store_sem.at[i])
-        for i, (src, dst) in enumerate([(lo, lo_h), (ig, ig_h), (agf, pg_h)])
-    ]
-
     start_zscatter(0)
 
     @pl.when(tm < n_tm - 1)
@@ -353,7 +356,6 @@
     lax.fori_loop(0, steps // 2, finish, 0)
     start_zgather(1)
     lax.fori_loop(steps // 2, steps, finish, 0)
-    stores[1].start()
 
     @pl.when(tm > 0)
     def _():
@@ -396,17 +398,18 @@
         when(me < owners, own_sum)
 
     attend(0, add, (steps + 1) // 2, steps)
-    stores[0].start()
 
     @pl.when(tm < n_tm - 1)
     def _():
-        fwd.wait_send()
+        for copy in fwd:
+            copy.wait_send()
         for halo in halos:
             halo.wait_send()
 
     @pl.when(tm > 0)
     def _():
-        rev.wait_send()
+        for copy in rev:
+            copy.wait_send()
 
     for turn in range(2):
         for copy in zscatter[turn] + zgather[turn]:
@@ -416,12 +419,10 @@
     for half in range(2):
         for cond, copy in gather[half]:
             when(cond, copy.wait_recv)
-    stores[2].start()
+    pg_out[...] = agf[...]
     for half in range(2):
         for _, copy in gather[half]:
             when(me < owners, copy.wait_send)
-    for store in stores:
-        store.wait()
 
 
 def hand_out(lo_ref, ig_ref, pg_ref, lo_out, ig_out, pg_out, pg, sem):
@@ -464,7 +465,6 @@
     chunk = share // owners
     zrows = rows // n_z
     hbm = pl.BlockSpec(memory_space=pltpu.HBM)
-    anywhere = pl.BlockSpec(memory_space=pl.ANY)
     vmem = pl.BlockSpec(memory_space=pltpu.VMEM)
     smem = pl.BlockSpec(memory_space=pltpu.SMEM)
 
@@ -475,17 +475,17 @@
     layer_out, input_grad, proj_grad = pl.pallas_call(
         functools.partial(kernel, sizes),
         out_shape=(
-            jax.ShapeDtypeStruct((rows, width), BF),
-            jax.ShapeDtypeStruct((rows, width), BF),
-            jax.ShapeDtypeStruct((2, share, states), BF),
+            v((rows, width)),
+            v((rows, width)),
+            v((2, share, states)),
         ),
         in_specs=[hbm, hbm, hbm, hbm, vmem, hbm, hbm, hbm, hbm, smem],
-        out_specs=(anywhere, anywhere, anywhere),
+        out_specs=(vmem, vmem, vmem),
         scratch_shapes=[
             v((rows, model)), v((model, 2 * states)),
             v((rows, width)), v((rows, width)), v((rows, width)),
             v((W + rows, width)), v((W + rows, width)),
-            v((rows, width)), v((rows, width)), v((share, rows)),
+            v((share, rows)),
             v((rows, width), F32), v((heads, rows), F32),
             v((rows, states)), v((rows, states)), v((rows, states)),
             v((rows, rows), F32), v((rows, rows), F32),
@@ -495,7 +495,7 @@
             v((states, width), F32), v((states, width)), v((states, width)),
             v((2, rows, states)), v((2, n_z - 1, zrows, states)), v((2, rows, states)),
             v((2, share, states)), v((2, group - 1, chunk, states)), v((2, share, states)),
-            dma((8,)), dma((3,)), dma((2,)), dma((2,)), dma((2,)), dma((2,)),
+            dma((8,)), dma((2, 2)), dma((2, 2)), dma((2,)), dma((2,)),
             dma((2, n_z - 1)), dma((2, n_z - 1)), dma((2, n_z - 1)), dma((2, n_z - 1)),
             dma((2, group - 1)), dma((2, group - 1)), dma((2, group - 1)), dma((2, group - 1)),
         ],
@@ -516,7 +516,7 @@
         in_specs=[vmem, vmem, vmem],
         out_specs=(hbm, hbm, hbm),
         scratch_shapes=[v((share, 2 * states), F32), dma((3,))],
-        compiler_params=pltpu.CompilerParams(vmem_limit_bytes=60 * 1024 * 1024),
+        compiler_params=pltpu.CompilerParams(vmem_limit_bytes=8 * 1024 * 1024),
     )(layer_out, input_grad, proj_grad)
     return layer_out[None], input_grad[None], proj_grad
 

time: 35.5 us -> 33.9 us (0.955)
  Pallas kernels: 34.6 us -> 33 us
    pallas_call x1, Pallas kernels: 2.43 us -> 1.17 us  [on_device(): pl.pallas_call(hand_out, out_shape=(jax.ShapeDtypeStruct((rows, width), B...]
where the time goes in v5:
time: 33.9 us; the launch traced here: 33.6 us
  Pallas kernels  33 us (97%)
  between operations  0.64 us (2%)
    pallas_call x1, Pallas kernels, on_device(): pl.pallas_call(functools.partial(kernel, sizes), out_shape=(v((rows, widt...  31.8 us
    pallas_call x1, Pallas kernels, on_device(): pl.pallas_call(hand_out, out_shape=(jax.ShapeDtypeStruct((rows, width), B...  1.17 us

profile of v5, /device:TPU:0, one launch (start us, length us, event | category | flops | bytes accessed | tf_op | source)
XLA Modules:
  0.0 33.6 jit_solution(16277479184945148571)
XLA Ops:
  0.6 31.8 %shard_map.121 = (bf16[256,1024]{1,0:T(8,128)(2,1)S(1)}, bf16[256,1024]{1,0:T(8,128)(2,1)S(1)}, bf16[2,512,128]{2,1,0:T(8,128)(2,1)S(1)}) custom-call(bf16[256,2048]{1,0:T(8,128)(2,1)} %bitcast.11, bf16[2048,128]{1,0:T(8,128)(2,1)} %pi_h.1, bf16[2048,128]{1,0:T(8,128)(2,1)} %po_h.1, bf16[256,1024]{1,0:T(8,128)(2,1)} %bitcast.12, f32[8,256]{1,0:T(8,128)} %bitcast.17, ...), custom_call_target="tpu_custom_call" | custom-call | tf_op jit(solution)/shard_map/pallas_call | solution.py:475
  32.5 1.2 %shard_map.122 = (bf16[256,1024]{1,0:T(8,128)(2,1)}, bf16[256,1024]{1,0:T(8,128)(2,1)}, f32[512,256]{1,0:T(8,128)}) custom-call(bf16[256,1024]{1,0:T(8,128)(2,1)S(1)} %get-tuple-element.9.lo_ref, bf16[256,1024]{1,0:T(8,128)(2,1)S(1)} %get-tuple-element.10.ig_ref, bf16[2,512,128]{2,1,0:T(8,128)(2,1)S(1)} %get-tuple-element.11.pg_ref), custom_call_target="tpu_custom_call" | custom-call | tf_op jit(solution)/shard_map/pallas_call | solution.py:509

commit v6 on v5

--- a/solution.py
+++ b/solution.py
@@ -32,7 +32,7 @@
     lat, proj, x, g, q, kx, vx, lat_t,
     cumb, cumt, b_s, c_s, cs_s, kern, wsum, xw, rg, inner, gx, att,
     f_fresh, f_in, f_out, r_fresh, r_in, r_out,
-    both, rz, zfull, term, rs, agf,
+    base, both, rz, zfull, term, rs, agf,
     load_sem, chain_send, chain_recv, halo_send, halo_recv,
     zs_send, zs_recv, zg_send, zg_recv, rs_send, rs_recv, ag_send, ag_recv,
 ):
@@ -173,6 +173,8 @@
     ]
     per = 4 if heads % 4 == 0 else heads
     steps = heads // per
+    pair = 2 if heads % 2 == 0 else 1
+    turns = heads // pair
     early_step(lambda place: place == 0)
     kern[...] = mm(cs_s[...], b_s[...], 1, 1)
     wsum[...] = jnp.zeros_like(wsum)
@@ -191,8 +193,8 @@
         early_step(lambda place: (place == i) & (i > 0))
 
         w00, w10, w11 = wsum[:dim, :dim], wsum[dim:, :dim], wsum[dim:, dim:]
-        for j in range(per):
-            h = i * per + j
+        for j in range(pair):
+            h = i * pair + j
             at = lanes(h)
             ct = cumt[pl.ds(h, 1), :]
             cb0, cb1 = cumb[:dim, at], cumb[dim:, at]
@@ -217,20 +219,22 @@
         wsum[dim:, dim:] = w11
         return 0
 
-    lax.fori_loop(0, steps, local_step, 0)
-
-    early_step(lambda place: place >= steps)
+    lax.fori_loop(0, turns, local_step, 0)
+
+    early_step(lambda place: place >= turns)
 
     weigh = (wsum[...] * scale).astype(BF)
+    base[1] = mm(weigh, b_s[...])
+    base[0] = mm(weigh, c_s[...], 0, 0)
     zscatter, zgather, scatter, gather = [[], []], [[], []], [[], []], [[], []]
     mine = pl.ds(pl.multiple_of(z * zrows, zrows), zrows)
     cols = pl.ds(pl.multiple_of(z * share, share), share)
 
     def fill_c():
-        both[1] = (mm(weigh, b_s[...]) + mm(rg[...], f_in[...], 1, 1) * scale).astype(BF)
+        both[1] = (base[1] + mm(rg[...], f_in[...], 1, 1) * scale).astype(BF)
 
     def fill_b():
-        both[0] = (mm(weigh, c_s[...], 0, 0) + mm(xw[...], r_in[...], 1, 1)).astype(BF)
+        both[0] = (base[0] + mm(xw[...], r_in[...], 1, 1)).astype(BF)
 
     def start_zscatter(turn):
         c_now = early_fwd if turn == 0 else jnp.logical_not(early_fwd)
@@ -493,7 +497,7 @@
             v((rows, width), F32), v((rows, width), F32), v((rows, width), F32),
             v((states, width), F32), v((states, width)), v((states, width)),
             v((states, width), F32), v((states, width)), v((states, width)),
-            v((2, rows, states)), v((2, n_z - 1, zrows, states)), v((2, rows, states)),
+            v((2, rows, states), F32), v((2, rows, states)), v((2, n_z - 1, zrows, states)), v((2, rows, states)),
             v((2, share, states)), v((2, group - 1, chunk, states)), v((2, share, states)),
             dma((8,)), dma((2, 2)), dma((2, 2)), dma((2,)), dma((2,)),
             dma((2, n_z - 1)), dma((2, n_z - 1)), dma((2, n_z - 1)), dma((2, n_z - 1)),

time: 33.9 us -> 33.8 us (level)
  no operation moved by 1% of the time
where the time goes in v6:
time: 33.8 us; the launch traced here: 33.6 us
  Pallas kernels  32.9 us (97%)
  between operations  0.64 us (2%)
    pallas_call x1, Pallas kernels, on_device(): pl.pallas_call(functools.partial(kernel, sizes), out_shape=(v((rows, widt...  31.8 us
    pallas_call x1, Pallas kernels, on_device(): pl.pallas_call(hand_out, out_shape=(jax.ShapeDtypeStruct((rows, width), B...  1.17 us

profile of v6, /device:TPU:0, one launch (start us, length us, event | category | flops | bytes accessed | tf_op | source)
XLA Modules:
  0.0 33.6 jit_solution(14492878186882288421)
XLA Ops:
  0.6 31.8 %shard_map.121 = (bf16[256,1024]{1,0:T(8,128)(2,1)S(1)}, bf16[256,1024]{1,0:T(8,128)(2,1)S(1)}, bf16[2,512,128]{2,1,0:T(8,128)(2,1)S(1)}) custom-call(bf16[256,2048]{1,0:T(8,128)(2,1)} %bitcast.11, bf16[2048,128]{1,0:T(8,128)(2,1)} %pi_h.1, bf16[2048,128]{1,0:T(8,128)(2,1)} %po_h.1, bf16[256,1024]{1,0:T(8,128)(2,1)} %bitcast.12, f32[8,256]{1,0:T(8,128)} %bitcast.17, ...), custom_call_target="tpu_custom_call" | custom-call | tf_op jit(solution)/shard_map/pallas_call | solution.py:479
  32.4 1.2 %shard_map.122 = (bf16[256,1024]{1,0:T(8,128)(2,1)}, bf16[256,1024]{1,0:T(8,128)(2,1)}, f32[512,256]{1,0:T(8,128)}) custom-call(bf16[256,1024]{1,0:T(8,128)(2,1)S(1)} %get-tuple-element.9.lo_ref, bf16[256,1024]{1,0:T(8,128)(2,1)S(1)} %get-tuple-element.10.ig_ref, bf16[2,512,128]{2,1,0:T(8,128)(2,1)S(1)} %get-tuple-element.11.pg_ref), custom_call_target="tpu_custom_call" | custom-call | tf_op jit(solution)/shard_map/pallas_call | solution.py:513
